TPU v7x, 32 devices: a whole 2x2x4 slice. The times are simulated.
32 devices in a mesh: tensor: 4 (over x, core), expert: 4 (over z), dp: 2 (over y).
Axes of the slice: x: 2, y: 2, z: 4, core: 2. Of those that a mesh axis runs over, the one named last changes fastest.
Arguments:
- queries: bfloat16 [8, 256, 2, 4096], P(('dp', 'expert'), None, None, 'tensor'), parts along dimension 0, may hold values from -6 to 6
- keys: bfloat16 [8, 256, 2, 512], P(('dp', 'expert'), None, None, 'tensor'), parts along dimension 0, may hold values from -6 to 6
- values: bfloat16 [8, 256, 2, 512], P(('dp', 'expert'), None, None, 'tensor'), parts along dimension 0, may hold values from -12 to 12
- q_gain: float32 [128], replicated, may hold values from 0 to 7
- k_gain: float32 [128], replicated, may hold values from 0 to 7
- out_weight: bfloat16 [4096, 4096], P('tensor', 'expert'), may hold values from -0.09375 to 0.09375
- hidden_in: bfloat16 [8, 256, 2, 4096], P(('dp', 'expert'), 'tensor'), parts along dimension 0, may hold values from -3 to 3
- norm_gain: float32 [4096], replicated, may hold values from 0.1 to 1.9
- router: bfloat16 [4096, 16], replicated, may hold values from -4 to 4
- expert_ids: int32 [8, 256, 2, 8], P(('dp', 'expert'), 'tensor'), parts along dimension 0, may hold values from 0 to 15, all different within a row; in each aligned block of 128 rows (0 to 127, 128 to 255, ..., all dimensions but the last counted through in order) at most 65 rows name the same one
- w_gate: bfloat16 [16, 4096, 768], P(('tensor', 'expert')), may hold values from -0.09375 to 0.09375
- w_up: bfloat16 [16, 4096, 768], P(('tensor', 'expert')), may hold values from -0.09375 to 0.09375
- w_down: bfloat16 [16, 768, 4096], P(('tensor', 'expert')), may hold values from -0.21875 to 0.21875
Outputs:
- hidden_out: bfloat16 [8, 256, 2, 4096], P(('dp', 'expert'), 'tensor'), parts along dimension 0
There are 2 independent parts, one for each index of `dp`. A program takes and returns all parts, laid end to end along the dimension named above; an argument that names none is the same for every part. Nothing has to cross between parts.
Inputs may be any that keep to these rules, and one draw needn't show every extreme that they name: `expert_ids`: each row names 8 different experts; among the 128 rows of one device no expert is named by more than 65 rows, a bound that some block reaches.
All inputs are finite; a program needn't handle non-finite values.
Results may differ from a plain program's by a relative error of at most 0.03.
The roundings to bfloat16 on the way count: a program that leaves them out, or rounds other values in their place, can miss the bound.
Values may be sent and summed in bfloat16 or wider, within the bound.
A program may use at most 256 MiB of HBM per device.

v0:
```python
import jax
import jax.numpy as jnp
from jax import lax
from jax.sharding import PartitionSpec as P

theta_base = 1000000.0
eps_norm = 1e-06
neg_fill = -1e30


def head_norm(values_in, gain_vec):
    scale_row = lax.rsqrt(jnp.mean(values_in * values_in, axis=-1, keepdims=True) + eps_norm)
    return values_in * scale_row * gain_vec


def rotary(values_in, places):
    width_all = values_in.shape[-1]
    half_width = width_all // 2
    frequency = theta_base ** (-2.0 * jnp.arange(half_width, dtype=jnp.float32) / width_all)
    angles = places.astype(jnp.float32)[:, None] * frequency[None, :]
    tile_shape = (places.shape[0],) + (1,) * (values_in.ndim - 2) + (half_width,)
    cosine = jnp.cos(angles).reshape(tile_shape)
    sine_part = jnp.sin(angles).reshape(tile_shape)
    first_half = values_in[..., :half_width]
    second = values_in[..., half_width:]
    return jnp.concatenate(
        [first_half * cosine - second * sine_part, second * cosine + first_half * sine_part],
        axis=-1,
    )


def attend(
    carry_state,
    query_set,
    query_places,
    low_bound,
    high_bound,
    key_piece,
    value_piece,
    start_row,
    score_scale,
):
    piece_len = key_piece.shape[0]
    key_places = jnp.arange(piece_len, dtype=jnp.int32)

    def compute(carry_inner):
        max_old, total_old, accum_old = carry_inner
        scores = (
            jnp.einsum(
                "pskgd,nskd->skgpn", query_set, key_piece, preferred_element_type=jnp.float32
            )
            * score_scale
        )
        allowed = (
            (key_places[None, :] <= query_places[:, None])
            & (key_places[None, :] >= low_bound)
            & (key_places[None, :] < high_bound)
        )
        scores = jnp.where(allowed, scores, neg_fill)
        max_new = jnp.maximum(max_old, jnp.max(scores, axis=-1))
        weights = jnp.where(allowed, jnp.exp(scores - max_new[..., None]), 0.0)
        total_new = jnp.sum(weights, axis=-1)
        accum_new = jnp.einsum(
            "skgpn,nskd->skgpd",
            weights.astype(jnp.bfloat16),
            value_piece,
            preferred_element_type=jnp.float32,
        )
        return (max_new, total_new, accum_new)

    live_piece = (
        (start_row <= jnp.max(query_places))
        & (start_row < high_bound)
        & (start_row + piece_len > low_bound)
    )
    return lax.cond(live_piece, compute, lambda carry_inner: carry_inner, carry_state)


def on_device(
    queries,
    keys,
    values,
    q_gain,
    k_gain,
    out_weight,
    hidden_in,
    norm_gain,
    router,
    expert_ids,
    w_gate,
    w_up,
    w_down,
):
    split_count = lax.axis_size("expert")
    tensor_count = lax.axis_size("tensor")
    place_index = lax.axis_index("expert")
    block_len = queries.shape[1]
    seq_count = queries.shape[2]
    head_dim = q_gain.shape[0]
    head_count = queries.shape[3] // head_dim
    kv_count = keys.shape[3] // head_dim
    group_size = head_count // kv_count
    score_scale = head_dim ** (-0.5)
    offsets = jnp.arange(block_len, dtype=jnp.int32)
    q_places = place_index * block_len + offsets
    q_field = queries[0].astype(jnp.float32).reshape(block_len, seq_count, head_count, head_dim)
    q_ready = (
        rotary(head_norm(q_field, q_gain), q_places)
        .astype(jnp.bfloat16)
        .reshape(block_len, seq_count, kv_count, group_size, head_dim)
    )
    k_field = keys[0].astype(jnp.float32).reshape(block_len, seq_count, kv_count, head_dim)
    k_ready = rotary(head_norm(k_field, k_gain), q_places).astype(jnp.bfloat16)
    v_ready = values[0].reshape(block_len, seq_count, kv_count, head_dim)
    stat_shape = (seq_count, kv_count, group_size, block_len)
    fresh_state = (
        jnp.full(stat_shape, neg_fill, jnp.float32),
        jnp.zeros(stat_shape, jnp.float32),
        jnp.zeros(stat_shape + (head_dim,), jnp.float32),
    )
    own_high = place_index * block_len + block_len
    folded = attend(
        fresh_state,
        q_ready,
        q_places,
        0,
        own_high,
        lax.all_gather(k_ready, "expert", axis=0, tiled=True),
        lax.all_gather(v_ready, "expert", axis=0, tiled=True),
        jnp.int32(0),
        score_scale,
    )
    max_all, total_all, accum_all = folded
    attended = (accum_all / total_all[..., None]).astype(jnp.bfloat16)
    attn_rows = jnp.transpose(attended, (3, 0, 1, 2, 4)).reshape(
        block_len * seq_count, head_count * head_dim
    )
    partial_value = jnp.dot(
        attn_rows,
        lax.all_gather(out_weight, "expert", axis=1, tiled=True),
        preferred_element_type=jnp.float32,
    )
    mixed_rows = lax.psum_scatter(
        partial_value.astype(jnp.bfloat16), "tensor", scatter_dimension=0, tiled=True
    ).astype(jnp.float32)
    d_model = hidden_in.shape[3]
    row_count = hidden_in.shape[1] * seq_count
    stream = (hidden_in.reshape(row_count, d_model).astype(jnp.float32) + mixed_rows).astype(
        jnp.bfloat16
    )
    stream_f = stream.astype(jnp.float32)
    normed = (
        stream_f
        * lax.rsqrt(jnp.mean(stream_f * stream_f, axis=-1, keepdims=True) + eps_norm)
        * norm_gain
    ).astype(jnp.bfloat16)
    logits = jnp.dot(normed, router, preferred_element_type=jnp.float32)
    local_experts = w_gate.shape[0]
    experts = local_experts * tensor_count * split_count
    top_count = expert_ids.shape[3]
    chosen = expert_ids.reshape(row_count, top_count)
    catalog = jnp.arange(experts, dtype=jnp.int32)
    chosen_mask = chosen[:, :, None] == catalog[None, None, :]
    picked = jnp.sum(jnp.where(chosen_mask, logits[:, None, :], 0.0), axis=-1)
    gate_weights = jax.nn.softmax(picked, axis=-1)
    flat_ids = chosen.reshape(row_count * top_count)
    hit_table = (flat_ids[:, None] == catalog[None, :]).astype(jnp.int32)
    slot_index = jnp.sum((jnp.cumsum(hit_table, axis=0) - hit_table) * hit_table, axis=1)
    capacity = max(2, row_count * top_count // experts + 1)
    sources = jnp.repeat(normed, top_count, axis=0)
    outgoing = (
        jnp.zeros((experts, capacity, d_model), jnp.bfloat16).at[flat_ids, slot_index].set(sources)
    )
    arrived = lax.all_to_all(
        outgoing, ("tensor", "expert"), split_axis=0, concat_axis=0, tiled=True
    )
    lane_rows = arrived.reshape(-1, local_experts, arrived.shape[1], d_model)
    gate_part = jnp.einsum("nlcd,ldf->nlcf", lane_rows, w_gate, preferred_element_type=jnp.float32)
    up_part = jnp.einsum("nlcd,ldf->nlcf", lane_rows, w_up, preferred_element_type=jnp.float32)
    inner_act = (jax.nn.silu(gate_part) * up_part).astype(jnp.bfloat16)
    done_rows = jnp.einsum(
        "nlcf,lfd->nlcd", inner_act, w_down, preferred_element_type=jnp.float32
    ).astype(jnp.bfloat16)
    returned = lax.all_to_all(
        done_rows.reshape(arrived.shape),
        ("tensor", "expert"),
        split_axis=0,
        concat_axis=0,
        tiled=True,
    )
    landed = returned[flat_ids, slot_index].reshape(row_count, top_count, d_model)
    blended = jnp.sum(gate_weights[:, :, None] * landed.astype(jnp.float32), axis=1)
    final_rows = (stream_f + blended).astype(jnp.bfloat16)
    return final_rows.reshape(hidden_in.shape)


def solution(mesh):
    return jax.shard_map(
        on_device,
        mesh=mesh,
        in_specs=(
            P(("dp", "expert"), None, None, "tensor"),
            P(("dp", "expert"), None, None, "tensor"),
            P(("dp", "expert"), None, None, "tensor"),
            P(),
            P(),
            P("tensor", "expert"),
            P(("dp", "expert"), "tensor", None, None),
            P(),
            P(),
            P(("dp", "expert"), "tensor", None, None),
            P(("tensor", "expert"), None, None),
            P(("tensor", "expert"), None, None),
            P(("tensor", "expert"), None, None),
        ),
        out_specs=P(("dp", "expert"), "tensor", None, None),
        check_vma=False,
    )
```

profile of v0, /device:TPU:0, one launch (start us, length us, event | category | flops | bytes accessed | tf_op | source)
XLA Modules:
  0.0 786.0 jit_solution(15736237788937209220)
XLA Ops:
  6.5 0.7 all-gather.3.cloned.1.call-update
  7.3 2.4 copy.42
  10.9 0.9 copy.43
  12.5 1.1 fusion.45
  13.6 1.1 fusion.46
  15.9 27.7 %all_gather.9 = bf16[1024,2,1,128]{3,0,1,2:T(8,128)(2,1)S(1)} all-gather(bf16[256,2,1,128]{3,0,1,2:T(8,128)(2,1)S(1)} %pad_maximum_fusion.1), channel_id=1, replica_groups=mesh['tensor'=4,'expert'=4,'dp'=2] {'expert'}, dimensions={0}, use_global_device_ids=true | all-gather | bytes 655360 | tf_op jit(solution)/shard_map/all_gather | solution.py:128
  43.7 23.4 %all-gather = bf16[1,1024,2,128]{3,1,2,0:T(8,128)(2,1)} all-gather(bf16[1,256,2,128]{3,1,2,0:T(8,128)(2,1)S(1)} %copy.43), channel_id=2, replica_groups=mesh['tensor'=4,'expert'=4,'dp'=2] {'expert'}, dimensions={1}, use_global_device_ids=true | all-gather | bytes 655360 | tf_op jit(solution)/shard_map/all_gather | solution.py:129
  67.1 25.3 %conditional.1 = (f32[2,1,8,256]{3,2,0,1:T(8,128)S(1)}, f32[2,1,8,256,128]{4,3,2,0,1:T(8,128)S(1)}) conditional(s32[]{:T(128)} %convert_element_type.110, () %tuple.13, (s32[1024]{0:T(1024)S(1)}, s32[256]{0:T(256)S(1)}, s32[1024]{0:T(1024)S(1)}, s32[]{:T(128)}, s32[1024]{0:T(1024)S(1)}, /*index=5*/bf16[1024,2,1,128]{3,0,1,2:T(8,128)(2,1)S(1)}, ...), branch_computations={%region_3.0_spmd, %region_4.7_spmd} | conditional | flops 2202793984 | bytes 55690260 | solution.py:76
  67.1 0.9 and_and_fusion
  68.0 7.2 fusion
  75.2 9.0 %fusion.7 = f32[2,1,8,256,128]{4,3,2,0,1:T(8,128)S(1)} fusion(f32[2,1024,256,8]{2,1,3,0:T(8,128)} %get-tuple-element.50, f32[2,8,256]{2,1,0:T(8,128)S(1)} %broadcast_maximum_fusion, pred[256,1024]{0,1:T(8,128)(4,1)S(1)} %and_and_fusion, bf16[1024,2,1,128]{3,0,1,2:T(8,128)(2,1)} %get-tuple-element.26), kind=kOutput, calls=%fused_computation.10 | convolution fusion | flops 1094713344 | bytes 19677184 | tf_op jit(solution)/shard_map/cond/branch_1_fun/skgpn,nskd->skgpd/dot_general | solution.py:63
  84.2 8.1 %fusion.2 = f32[2,8,256]{2,1,0:T(8,128)S(1)} fusion(f32[2,1024,256,8]{2,1,3,0:T(8,128)} %get-tuple-element.50, f32[2,8,256]{2,1,0:T(8,128)S(1)} %broadcast_maximum_fusion, pred[256,1024]{0,1:T(8,128)(4,1)S(1)} %and_and_fusion), kind=kLoop, calls=%fused_computation.6 | loop fusion | flops 20967424 | bytes 17072128 | tf_op jit(solution)/shard_map/cond/branch_1_fun/reduce_sum | solution.py:62
  92.4 0.7 fusion.42
  93.8 81.0 %all-gather.3.cloned.1.call-done = bf16[1024,4096]{1,0:T(8,128)(2,1)} async-done(((bf16[1024,1024]{1,0:T(8,128)(2,1)}), bf16[1024,4096]{1,0:T(8,128)(2,1)}) %all-gather.3.cloned.1.call-update) | async-done | bytes 8388624 | tf_op jit(solution)/shard_map/all_gather | solution.py:140
  174.8 9.5 %convolution_convert_fusion.1 = bf16[512,4096]{1,0:T(8,128)(2,1)} fusion(bf16[1024,4096]{1,0:T(8,128)(2,1)} %all-gather.3.cloned.1.call-done, bf16[64,8,8,128]{3,2,1,0:T(8,128)(2,1)S(1)} %bitcast.149), kind=kOutput, calls=%fused_computation.33 | convolution fusion | flops 4297064448 | bytes 13631488 | tf_op jit(solution)/shard_map/dot_general | solution.py:138
  184.9 1.5 reshape.350
  186.4 4.5 reduce-window.6
  191.6 37.6 %reduce-scatter.2.cloned.1.call-done = bf16[128,4096]{1,0:T(8,128)(2,1)} async-done(((bf16[512,4096]{1,0:T(8,128)(2,1)}), bf16[128,4096]{1,0:T(8,128)(2,1)}) %reduce-scatter.2.cloned.1.call-update) | async-done | bytes 1048592 | tf_op jit(solution)/shard_map/reduce_scatter | solution.py:143
  229.2 2.3 fusion.35
  231.8 16.3 %scatter_custom_fusion = bf16[1040,4096]{1,0:T(8,128)(2,1)} fusion(s32[1024]{0:T(1024)S(1)} %broadcast_select_fusion, bf16[]{:T(256)} %constant.26.clone.1, bf16[128,4096]{1,0:T(8,128)(2,1)S(1)} %fusion.37), kind=kCustom, calls=%fused_computation.25 | custom fusion | bytes 9568258
  248.1 11.8 %copy.69 = bf16[65,16,4096]{2,0,1:T(8,128)(2,1)} copy(bf16[65,16,4096]{2,1,0:T(8,128)(2,1)} %bitcast.145) | data formatting | bytes 17039360
  259.9 212.3 %all_to_all.10 = bf16[16,65,4096]{2,1,0:T(8,128)(2,1)S(1)} all-to-all(bf16[16,65,4096]{2,1,0:T(8,128)(2,1)} %bitcast.144), channel_id=1, replica_groups=mesh['tensor'=4,'expert'=4,'dp'=2] {'tensor','expert'}, dimensions={0} | all-to-all | bytes 17039360 | tf_op jit(solution)/shard_map/all_to_all | solution.py:174
  472.3 12.0 %fusion.21 = f32[16,65,768]{2,1,0:T(8,128)S(1)} fusion(bf16[16,65,4096]{2,1,0:T(8,128)(2,1)S(1)} %all_to_all.10, bf16[1,4096,768]{2,1,0:T(8,128)(2,1)} %param.26), kind=kOutput, calls=%fused_computation.29 | convolution fusion | flops 6543114240 | bytes 18006016 | tf_op jit(solution)/shard_map/nlcd,ldf->nlcf/dot_general | solution.py:179
  484.3 9.3 %fusion.27 = bf16[16,1,65,768]{3,2,0,1:T(8,128)(2,1)} fusion(f32[16,65,768]{2,1,0:T(8,128)S(1)} %fusion.21, bf16[16,65,4096]{2,1,0:T(8,128)(2,1)S(1)} %all_to_all.10, bf16[1,4096,768]{2,1,0:T(8,128)(2,1)S(1)} %bitcast.157), kind=kOutput, calls=%fused_computation.37 | convolution fusion | flops 6547906560 | bytes 19603456 | tf_op jit(solution)/shard_map/nlcd,ldf->nlcf/dot_general | solution.py:178
  493.6 11.4 %convolution_convert_fusion = bf16[16,65,4096]{2,1,0:T(8,128)(2,1)} fusion(bf16[1,768,4096]{2,1,0:T(8,128)(2,1)S(1)} %bitcast.159, bf16[16,1,65,768]{3,2,0,1:T(8,128)(2,1)} %fusion.27), kind=kOutput, calls=%fused_computation.27 | convolution fusion | flops 6547374080 | bytes 16408576 | tf_op jit(solution)/shard_map/nlcf,lfd->nlcd/dot_general | solution.py:181
  505.1 4.9 all-to-all-start.1
  510.7 206.1 %all-to-all-done.1 = bf16[16,65,4096]{2,1,0:T(8,128)(2,1)} async-done(((bf16[16,65,4096]{2,1,0:T(8,128)(2,1)}), bf16[16,65,4096]{2,1,0:T(8,128)(2,1)}, u32[]{:S(2)}, u32[]{:S(2)}) %all-to-all-start.1) | async-done | bytes 8519712 | tf_op jit(solution)/shard_map/all_to_all | solution.py:184
  716.8 11.7 %copy.55 = bf16[16,65,4096]{2,0,1:T(8,128)(2,1)} copy(bf16[16,65,4096]{2,1,0:T(8,128)(2,1)} %all-to-all-done.1) | data formatting | bytes 17039360 | tf_op jit(solution)/shard_map/all_to_all | solution.py:184
  728.5 33.9 %gather_fusion = bf16[1024,4096]{1,0:T(8,128)(2,1)} fusion(bf16[16,65,4096]{2,0,1:T(8,128)(2,1)} %copy.55, s32[1024]{0:T(1024)S(1)} %bitcast.143), kind=kCustom, calls=%fused_computation | custom fusion | bytes 16785408 | tf_op jit(solution)/shard_map/gather | solution.py:191
  762.4 13.2 %fusion.17 = f32[128,4096]{1,0:T(8,128)} fusion(bf16[1024,4096]{1,0:T(8,128)(2,1)} %gather_fusion, f32[128,8]{1,0:T(8,128)S(1)} %copy.48), kind=kLoop, calls=%fused_computation.23 | loop fusion | flops 12058624 | bytes 10489856 | tf_op jit(solution)/shard_map/reduce_sum | solution.py:192
  775.6 1.8 fusion.38
  777.5 1.5 reshape.345
  (70 shorter events, 5.3 us)
Async XLA Ops:
  6.5 503.5 %copy-start = (bf16[4096,16]{0,1:T(8,128)(2,1)S(1)}, bf16[4096,16]{0,1:T(8,128)(2,1)}, u32[]{:S(2)}) copy-start(bf16[4096,16]{0,1:T(8,128)(2,1)} %param.23) | copy-start | bytes 393220
  6.5 8.6 %copy-start.6 = (f32[128]{0:T(128)S(1)}, f32[128]{0:T(128)}, u32[]{:S(2)}) copy-start(f32[128]{0:T(128)} %param.18) | copy-start | bytes 1540
  6.5 168.3 %all-gather.3.cloned.1.call-start = ((), (), s32[]{:S(2)}) async-start(), calls=%async_computation.3 | async-start | bytes 10485760 | tf_op jit(solution)/shard_map/all_gather | solution.py:140
  7.3 221.9 %reduce-scatter.2.cloned.1.call-start = ((), (), s32[]{:S(2)}) async-start(), calls=%async_computation.4 | async-start | bytes 5242880 | tf_op jit(solution)/shard_map/reduce_scatter | solution.py:143
  174.8 9.5 %copy-start.3 = (s32[1,64,2,8]{1,3,2,0:T(8,128)S(1)}, s32[1,64,2,8]{1,3,2,0:T(8,128)}, u32[]{:S(2)}) copy-start(s32[1,64,2,8]{1,3,2,0:T(8,128)} %param.24) | copy-start | bytes 12292
  174.8 10.0 %copy-start.1 = (bf16[1,64,2,4096]{3,2,1,0:T(2,128)(2,1)S(1)}, bf16[1,64,2,4096]{3,2,1,0:T(2,128)(2,1)}, u32[]{:S(2)}) copy-start(bf16[1,64,2,4096]{3,2,1,0:T(2,128)(2,1)} %param.21) | copy-start | bytes 3145732
  184.3 7.1 copy-start.5
  184.3 7.2 copy-start.4
  184.3 47.2 %copy-start.2 = (f32[4096]{0:T(1024)S(1)}, f32[4096]{0:T(1024)}, u32[]{:S(2)}) copy-start(f32[4096]{0:T(1024)} %param.22) | copy-start | bytes 49156
  259.9 224.4 %slice-start = ((s8[6291456]{0:T(1024)(128)(4,1)}), s8[4194304]{0:T(1024)(128)(4,1)S(1)}, s32[]{:S(2)}) async-start(s8[6291456]{0:T(1024)(128)(4,1)} %bitcast.156), calls=%async_computation.5 | async-start | bytes 8388608
  472.3 12.0 %slice-start.1 = ((s8[6291456]{0:T(1024)(128)(4,1)}), s8[2097152]{0:T(1024)(128)(4,1)S(1)}, s32[]{:S(2)}) async-start(s8[6291456]{0:T(1024)(128)(4,1)} %bitcast.156), calls=%async_computation.6 | async-start | bytes 4194304
  472.3 21.4 %slice-start.2 = ((s8[6291456]{0:T(1024)(128)(4,1)}), s8[4194304]{0:T(1024)(128)(4,1)S(1)}, s32[]{:S(2)}) async-start(s8[6291456]{0:T(1024)(128)(4,1)} %bitcast.158), calls=%async_computation.7 | async-start | bytes 8388608
  484.3 9.3 %slice-start.3 = ((s8[6291456]{0:T(1024)(128)(4,1)}), s8[2097152]{0:T(1024)(128)(4,1)S(1)}, s32[]{:S(2)}) async-start(s8[6291456]{0:T(1024)(128)(4,1)} %bitcast.158), calls=%async_computation.8 | async-start | bytes 4194304
  505.1 211.7 %all-to-all-start.1 = ((bf16[16,65,4096]{2,1,0:T(8,128)(2,1)}), bf16[16,65,4096]{2,1,0:T(8,128)(2,1)}, u32[]{:S(2)}, u32[]{:S(2)}) async-start(bf16[16,65,4096]{2,1,0:T(8,128)(2,1)} %convolution_convert_fusion), calls=%async_computation.2 | async-start | bytes 18874368 | tf_op jit(solution)/shard_map/all_to_all | solution.py:184
Sparse Core Ops, SparseCore 0:
  8.9 165.8 all-gather.2
  184.5 44.6 reduce-scatter.1
where the time goes:
time: 793 us; the launch traced here: 786 us
  waiting for transfers between devices  325 us (41%)
  blocking collectives  264 us (33%)
  local copies, waits for them, and re-layouts  81.9 us (10%)
  matrix products  58.7 us (7%)
  other arithmetic  36.6 us (5%)
  between operations  14.6 us (2%)
    all_to_all x1, blocking collectives, on_device(): lax.all_to_all(outgoing, ('tensor', 'expert'), split_axis=0, concat_axis=...  212 us
    all_to_all x1, waiting for transfers between devices, on_device(): lax.all_to_all(done_rows.reshape(arrived.shape), ('tensor', 'expert'), sp...  206 us
    all_gather x1, waiting for transfers between devices, on_device(): lax.all_gather(out_weight, 'expert', axis=1, tiled=True)  81 us
    reduce_scatter x1, waiting for transfers between devices, on_device(): lax.psum_scatter(partial_value.astype(jnp.bfloat16), 'tensor', scatter_di...  37.6 us
    gather x1, local copies, waits for them, and re-layouts, on_device(): returned[flat_ids, slot_index].reshape(row_count, top_count, d_model)  33.9 us
    unnamed x27, local copies, waits for them, and re-layouts  31.6 us
    all_gather x1, blocking collectives, on_device(): lax.all_gather(k_ready, 'expert', axis=0, tiled=True)  27.7 us
    all_gather x1, blocking collectives, on_device(): lax.all_gather(v_ready, 'expert', axis=0, tiled=True)  23.4 us
  transfers between devices with their start and end apart: 3, of which 3 were waited for; matrix products, arithmetic and copies ran while one was open for 5% of the time, Pallas kernels for 0%

commit v1 on v0

--- a/solution.py
+++ b/solution.py
@@ -6,6 +6,7 @@
 theta_base = 1000000.0
 eps_norm = 1e-06
 neg_fill = -1e30
+chunk_count = 2
 
 
 def head_norm(values_in, gain_vec):
@@ -119,14 +120,17 @@
         jnp.zeros(stat_shape + (head_dim,), jnp.float32),
     )
     own_high = place_index * block_len + block_len
+    kv_pack = lax.all_gather(
+        jnp.concatenate([k_ready, v_ready], axis=-1), "expert", axis=0, tiled=True
+    )
     folded = attend(
         fresh_state,
         q_ready,
         q_places,
         0,
         own_high,
-        lax.all_gather(k_ready, "expert", axis=0, tiled=True),
-        lax.all_gather(v_ready, "expert", axis=0, tiled=True),
+        kv_pack[..., :head_dim],
+        kv_pack[..., head_dim:],
         jnp.int32(0),
         score_scale,
     )
@@ -135,11 +139,12 @@
     attn_rows = jnp.transpose(attended, (3, 0, 1, 2, 4)).reshape(
         block_len * seq_count, head_count * head_dim
     )
-    partial_value = jnp.dot(
-        attn_rows,
-        lax.all_gather(out_weight, "expert", axis=1, tiled=True),
-        preferred_element_type=jnp.float32,
-    )
+    share = out_weight.shape[1] // lax.axis_size("dp")
+    own_share = lax.dynamic_slice_in_dim(out_weight, lax.axis_index("dp") * share, share, 1)
+    weight_parts = lax.all_gather(own_share, ("expert", "dp"), axis=0, tiled=False)
+    partial_value = jnp.einsum(
+        "rc,gcn->rgn", attn_rows, weight_parts, preferred_element_type=jnp.float32
+    ).reshape(attn_rows.shape[0], -1)
     mixed_rows = lax.psum_scatter(
         partial_value.astype(jnp.bfloat16), "tensor", scatter_dimension=0, tiled=True
     ).astype(jnp.float32)
@@ -154,42 +159,43 @@
         * lax.rsqrt(jnp.mean(stream_f * stream_f, axis=-1, keepdims=True) + eps_norm)
         * norm_gain
     ).astype(jnp.bfloat16)
-    logits = jnp.dot(normed, router, preferred_element_type=jnp.float32)
     local_experts = w_gate.shape[0]
-    experts = local_experts * tensor_count * split_count
+    device_count = tensor_count * split_count
+    experts = local_experts * device_count
     top_count = expert_ids.shape[3]
-    chosen = expert_ids.reshape(row_count, top_count)
+    spread = ("tensor", "expert")
+    chosen = lax.all_gather(expert_ids.reshape(row_count, top_count), spread, axis=0)
     catalog = jnp.arange(experts, dtype=jnp.int32)
-    chosen_mask = chosen[:, :, None] == catalog[None, None, :]
-    picked = jnp.sum(jnp.where(chosen_mask, logits[:, None, :], 0.0), axis=-1)
-    gate_weights = jax.nn.softmax(picked, axis=-1)
-    flat_ids = chosen.reshape(row_count * top_count)
-    hit_table = (flat_ids[:, None] == catalog[None, :]).astype(jnp.int32)
-    slot_index = jnp.sum((jnp.cumsum(hit_table, axis=0) - hit_table) * hit_table, axis=1)
-    capacity = max(2, row_count * top_count // experts + 1)
-    sources = jnp.repeat(normed, top_count, axis=0)
-    outgoing = (
-        jnp.zeros((experts, capacity, d_model), jnp.bfloat16).at[flat_ids, slot_index].set(sources)
-    )
-    arrived = lax.all_to_all(
-        outgoing, ("tensor", "expert"), split_axis=0, concat_axis=0, tiled=True
-    )
-    lane_rows = arrived.reshape(-1, local_experts, arrived.shape[1], d_model)
-    gate_part = jnp.einsum("nlcd,ldf->nlcf", lane_rows, w_gate, preferred_element_type=jnp.float32)
-    up_part = jnp.einsum("nlcd,ldf->nlcf", lane_rows, w_up, preferred_element_type=jnp.float32)
-    inner_act = (jax.nn.silu(gate_part) * up_part).astype(jnp.bfloat16)
-    done_rows = jnp.einsum(
-        "nlcf,lfd->nlcd", inner_act, w_down, preferred_element_type=jnp.float32
-    ).astype(jnp.bfloat16)
-    returned = lax.all_to_all(
-        done_rows.reshape(arrived.shape),
-        ("tensor", "expert"),
-        split_axis=0,
-        concat_axis=0,
-        tiled=True,
-    )
-    landed = returned[flat_ids, slot_index].reshape(row_count, top_count, d_model)
-    blended = jnp.sum(gate_weights[:, :, None] * landed.astype(jnp.float32), axis=1)
+    first_expert = (lax.axis_index("tensor") * split_count + place_index) * local_experts
+    piece_rows = row_count // chunk_count
+    blended = []
+    for chunk in range(chunk_count):
+        span = slice(chunk * piece_rows, (chunk + 1) * piece_rows)
+        rows = lax.all_gather(normed[span], spread, axis=0, tiled=True)
+        ids = chosen[:, span].reshape(-1, top_count)
+        named = jnp.any(ids[:, :, None] == catalog[None, None, :], axis=1)
+        logits = jnp.dot(rows, router, preferred_element_type=jnp.float32)
+        top_logit = jnp.max(jnp.where(named, logits, -jnp.inf), axis=-1, keepdims=True)
+        odds = jnp.where(named, jnp.exp(jnp.where(named, logits - top_logit, 0.0)), 0.0)
+        gates = odds / jnp.sum(odds, axis=-1, keepdims=True)
+        share_sum = 0.0
+        for local in range(local_experts):
+            gate_part = jnp.dot(rows, w_gate[local], preferred_element_type=jnp.float32)
+            up_part = jnp.dot(rows, w_up[local], preferred_element_type=jnp.float32)
+            inner_act = (jax.nn.silu(gate_part) * up_part).astype(jnp.bfloat16)
+            expert_rows = jnp.dot(
+                inner_act, w_down[local], preferred_element_type=jnp.float32
+            ).astype(jnp.bfloat16)
+            own_gate = jnp.sum(
+                jnp.where(catalog == first_expert + local, gates, 0.0), axis=-1, keepdims=True
+            )
+            share_sum = share_sum + own_gate * expert_rows.astype(jnp.float32)
+        blended.append(
+            lax.psum_scatter(
+                share_sum.astype(jnp.bfloat16), spread, scatter_dimension=0, tiled=True
+            )
+        )
+    blended = jnp.concatenate(blended, axis=0).astype(jnp.float32)
     final_rows = (stream_f + blended).astype(jnp.bfloat16)
     return final_rows.reshape(hidden_in.shape)
 

time: 793 us -> 652 us (0.82)
  blocking collectives: 264 us -> 32.3 us
  waiting for transfers between devices: 325 us -> 454 us
  local copies, waits for them, and re-layouts: 81.9 us -> 19.8 us
  matrix products: 58.7 us -> 101 us
  other arithmetic: 36.6 us -> 20.7 us
    all_to_all x1 -> x0, blocking collectives: 212 us -> none  [on_device(): lax.all_to_all(outgoing, ('tensor', 'expert'), split_axis=0, concat_axis=...]
    all_to_all x1 -> x0, waiting for transfers between devices: 206 us -> none  [on_device(): lax.all_to_all(done_rows.reshape(arrived.shape), ('tensor', 'expert'), sp...]
    reduce_scatter x0 -> x2, waiting for transfers between devices: none -> 179 us  [on_device(): lax.psum_scatter(share_sum.astype(jnp.bfloat16), spread, scatter_dimensio...]
    all_gather x1 -> x4, waiting for transfers between devices: 81 us -> 232 us  [the longest x2 112 us: on_device(): rows = lax.all_gather(normed[span], spread, axis=0, tiled=True)]
    dot_general x5 -> x9, matrix products: 42.6 us -> 79.2 us  [the longest x2 21 us: on_device(): up_part = jnp.dot(rows, w_up[local], preferred_element_type=jnp.float32)]
    gather x1 -> x0, local copies, waits for them, and re-layouts: 33.9 us -> none  [on_device(): returned[flat_ids, slot_index].reshape(row_count, top_count, d_model)]
    unnamed x27 -> x33, local copies, waits for them, and re-layouts: 31.6 us -> 2.16 us
    all_gather x2 -> x1, blocking collectives: 51.2 us -> 32.3 us  [on_device(): lax.all_gather(expert_ids.reshape(row_count, top_count), spread, axis=0)]
  transfers between devices with their start and end apart: 3 -> 7, of which waited for: 3 -> 7; matrix products, arithmetic and copies ran while one was open for 5% -> 12% of each run, Pallas kernels for 0% -> 0%
where the time goes in v1:
time: 652 us; the launch traced here: 643 us
  waiting for transfers between devices  454 us (70%)
  matrix products  101 us (15%)
  blocking collectives  32.3 us (5%)
  other arithmetic  20.7 us (3%)
  local copies, waits for them, and re-layouts  19.8 us (3%)
  between operations  14.9 us (2%)
    reduce_scatter x2, waiting for transfers between devices, on_device(): lax.psum_scatter(share_sum.astype(jnp.bfloat16), spread, scatter_dimensio...  179 us
    all_gather x2, waiting for transfers between devices, on_device(): rows = lax.all_gather(normed[span], spread, axis=0, tiled=True)  112 us
    all_gather x1, waiting for transfers between devices, on_device(): lax.all_gather(own_share, ('expert', 'dp'), axis=0, tiled=False)  93 us
    reduce_scatter x1, waiting for transfers between devices, on_device(): lax.psum_scatter(partial_value.astype(jnp.bfloat16), 'tensor', scatter_di...  42.4 us
    all_gather x1, blocking collectives, on_device(): lax.all_gather(expert_ids.reshape(row_count, top_count), spread, axis=0)  32.3 us
    all_gather x1, waiting for transfers between devices, on_device(): lax.all_gather(jnp.concatenate([k_ready, v_ready], axis=-1), 'expert', ax...  26.9 us
    dot_general x2, matrix products, on_device(): up_part = jnp.dot(rows, w_up[local], preferred_element_type=jnp.float32)  21 us
    dot_general x2, matrix products, on_device(): gate_part = jnp.dot(rows, w_gate[local], preferred_element_type=jnp.float32)  19.4 us
  transfers between devices with their start and end apart: 7, of which 7 were waited for; matrix products, arithmetic and copies ran while one was open for 12% of the time, Pallas kernels for 0%

profile of v1, /device:TPU:0, one launch (start us, length us, event | category | flops | bytes accessed | tf_op | source)
XLA Modules:
  0.0 643.2 jit_solution(12376345255636212959)
XLA Ops:
  7.7 1.1 fusion.46
  8.8 0.9 copy.86
  9.7 1.1 fusion.47
  11.9 1.1 constant_dynamic-slice_fusion
  13.1 1.1 copy.67
  15.7 26.9 %all-gather.6.cloned.1.call-done = bf16[1024,2,1,256]{3,0,1,2:T(8,128)(2,1)} async-done(((bf16[256,2,1,256]{3,0,1,2:T(8,128)(2,1)}), bf16[1024,2,1,256]{3,0,1,2:T(8,128)(2,1)}) %all-gather.6.cloned.1.call-update) | async-done | bytes 1048592 | tf_op jit(solution)/shard_map/all_gather | solution.py:123
  42.6 30.9 %conditional.1 = (f32[2,1,8,256]{3,2,0,1:T(8,128)S(1)}, f32[2,1,8,256,128]{4,3,2,0,1:T(8,128)}) conditional(s32[]{:T(128)} %convert_element_type.115, () %tuple.13, (s32[1024]{0:T(1024)S(1)}, s32[256]{0:T(256)S(1)}, s32[1024]{0:T(1024)S(1)}, s32[]{:T(128)}, s32[1024]{0:T(1024)S(1)}, /*index=5*/bf16[1024,2,1,256]{3,0,1,2:T(8,128)(2,1)}, ...), branch_computations={%region_3.0_spmd, %region_4.7_spmd} | conditional | flops 2202793984 | bytes 59884592 | solution.py:77
  43.5 8.6 %fusion = (f32[2,8,256]{2,1,0:T(8,128)S(1)}, f32[2,1024,256,8]{2,1,3,0:T(8,128)}) fusion(pred[256,1024]{0,1:T(8,128)(4,1)S(1)} %and_and_fusion, bf16[256,2,1,8,128]{0,4,3,1,2:T(8,128)(2,1)S(1)} %get-tuple-element.65, bf16[1024,2,1,256]{3,0,1,2:T(8,128)(2,1)} %get-tuple-element.25), kind=kOutput, calls=%fused_computation.2 | convolution fusion | flops 1086320640 | bytes 18628608 | tf_op jit(solution)/shard_map/cond/branch_1_fun/pskgd,nskd->skgpn/dot_general | solution.py:50
  52.1 13.2 %fusion.7 = f32[2,1,8,256,128]{4,3,2,0,1:T(8,128)} fusion(f32[2,1024,256,8]{2,1,3,0:T(8,128)} %get-tuple-element.71, f32[2,8,256]{2,1,0:T(8,128)S(1)} %broadcast_maximum_fusion, pred[256,1024]{0,1:T(8,128)(4,1)S(1)} %and_and_fusion, bf16[1024,2,1,256]{3,0,1,2:T(8,128)(2,1)S(1)} %copy-done.6), kind=kOutput, calls=%fused_computation.8 | convolution fusion | flops 1094713344 | bytes 19677184 | tf_op jit(solution)/shard_map/cond/branch_1_fun/skgpn,nskd->skgpd/dot_general | solution.py:64
  65.3 8.0 %fusion.2 = f32[2,8,256]{2,1,0:T(8,128)S(1)} fusion(f32[2,1024,256,8]{2,1,3,0:T(8,128)} %get-tuple-element.71, f32[2,8,256]{2,1,0:T(8,128)S(1)} %broadcast_maximum_fusion, pred[256,1024]{0,1:T(8,128)(4,1)S(1)} %and_and_fusion), kind=kLoop, calls=%fused_computation.4 | loop fusion | flops 20967424 | bytes 17072128 | tf_op jit(solution)/shard_map/cond/branch_1_fun/reduce_sum | solution.py:63
  73.5 1.9 fusion.41
  76.2 93.0 %all-gather.12.cloned.1.call-done = bf16[8192,512]{1,0:T(8,128)(2,1)} async-done(((bf16[1024,512]{1,0:T(8,128)(2,1)}), bf16[8192,512]{1,0:T(8,128)(2,1)}) %all-gather.12.cloned.1.call-update) | async-done | bytes 8388624 | tf_op jit(solution)/shard_map/all_gather | solution.py:144
  169.2 11.5 %copy.70 = bf16[8,512,1024]{2,1,0:T(8,128)(2,1)} copy(bf16[8,512,1024]{1,2,0:T(8,128)(2,1)} %bitcast.108) | data formatting | bytes 16777216 | tf_op jit(solution)/shard_map/rc,gcn->rgn/dot_general | solution.py:145
  180.7 9.6 %convolution_convert_fusion = bf16[512,4096]{1,0:T(8,128)(2,1)} fusion(bf16[4096,1024]{1,0:T(8,128)(2,1)} %bitcast.109, bf16[64,8,8,128]{3,2,1,0:T(8,128)(2,1)S(1)} %bitcast.110), kind=kOutput, calls=%fused_computation.34 | convolution fusion | flops 4297064448 | bytes 13631488 | tf_op jit(solution)/shard_map/rc,gcn->rgn/dot_general | solution.py:145
  190.7 42.4 %reduce-scatter.4.cloned.1.call-done = bf16[128,4096]{1,0:T(8,128)(2,1)} async-done(((bf16[512,4096]{1,0:T(8,128)(2,1)}), bf16[128,4096]{1,0:T(8,128)(2,1)}) %reduce-scatter.4.cloned.1.call-update) | async-done | bytes 1048592 | tf_op jit(solution)/shard_map/reduce_scatter | solution.py:148
  233.2 1.6 fusion.35
  235.1 1.1 fusion.52
  237.0 32.3 %all_gather.21 = s32[16,128,8]{1,2,0:T(8,128)S(1)} all-gather(s32[1,128,8]{1,2,0:T(8,128)S(1)} %copy.72), channel_id=1, replica_groups=mesh['tensor'=4,'expert'=4,'dp'=2] {'tensor','expert'}, dimensions={0}, use_global_device_ids=true | all-gather | bytes 69632 | tf_op jit(solution)/shard_map/all_gather | solution.py:167
  269.8 42.4 %all-gather.10.cloned.1.call-done = bf16[1024,4096]{1,0:T(8,128)(2,1)} async-done(((bf16[64,4096]{1,0:T(8,128)(2,1)}), bf16[1024,4096]{1,0:T(8,128)(2,1)}) %all-gather.10.cloned.1.call-update) | async-done | bytes 8388624 | tf_op jit(solution)/shard_map/all_gather | solution.py:174
  312.1 5.7 select_reduce_fusion.1
  317.8 69.8 %all-gather.8.cloned.1.call-done = bf16[1024,4096]{1,0:T(8,128)(2,1)} async-done(((bf16[64,4096]{1,0:T(8,128)(2,1)}), bf16[1024,4096]{1,0:T(8,128)(2,1)}) %all-gather.8.cloned.1.call-update) | async-done | bytes 8388624 | tf_op jit(solution)/shard_map/all_gather | solution.py:174
  387.6 5.8 select_reduce_fusion.3
  393.6 9.4 %fusion.23 = f32[1024,768]{1,0:T(8,128)S(1)} fusion(bf16[1024,4096]{1,0:T(8,128)(2,1)S(1)} %copy-done.2, bf16[1,4096,768]{2,1,0:T(8,128)(2,1)} %param.26), kind=kOutput, calls=%fused_computation.28 | convolution fusion | flops 6442450944 | bytes 17825792 | tf_op jit(solution)/shard_map/dot_general | solution.py:184
  403.0 7.0 %multiply_convert_fusion.3 = bf16[1024,768]{1,0:T(8,128)(2,1)S(1)} fusion(f32[1024,768]{1,0:T(8,128)S(1)} %fusion.23, bf16[1024,4096]{1,0:T(8,128)(2,1)S(1)} %copy-done.2, bf16[1,4096,768]{2,1,0:T(8,128)(2,1)S(1)} %bitcast.116), kind=kOutput, calls=%fused_computation.36 | convolution fusion | flops 6447169536 | bytes 19398656 | tf_op jit(solution)/shard_map/dot_general | solution.py:183
  410.0 8.9 %multiply_convert_fusion.1 = bf16[1024,4096]{1,0:T(8,128)(2,1)} fusion(f32[1024]{0:T(1024)S(1)} %get-tuple-element.66, bf16[1024,768]{1,0:T(8,128)(2,1)S(1)} %multiply_convert_fusion.3, bf16[1,768,4096]{2,1,0:T(8,128)(2,1)S(1)} %bitcast.118), kind=kOutput, calls=%fused_computation.23 | convolution fusion | flops 6459228160 | bytes 16257024 | tf_op jit(solution)/shard_map/dot_general | solution.py:186
  419.0 11.6 %fusion.21 = f32[1024,768]{1,0:T(8,128)S(1)} fusion(bf16[1024,4096]{1,0:T(8,128)(2,1)} %all-gather.10.cloned.1.call-done, bf16[1,4096,768]{2,1,0:T(8,128)(2,1)} %param.26), kind=kOutput, calls=%fused_computation.26 | convolution fusion | flops 6442450944 | bytes 17825792 | tf_op jit(solution)/shard_map/dot_general | solution.py:184
  430.7 12.4 %multiply_convert_fusion.2 = bf16[1024,768]{1,0:T(8,128)(2,1)S(1)} fusion(f32[1024,768]{1,0:T(8,128)S(1)} %fusion.21, bf16[1024,4096]{1,0:T(8,128)(2,1)} %all-gather.10.cloned.1.call-done, bf16[1,4096,768]{2,1,0:T(8,128)(2,1)} %param.25), kind=kOutput, calls=%fused_computation.35 | convolution fusion | flops 6447169536 | bytes 19398656 | tf_op jit(solution)/shard_map/dot_general | solution.py:183
  443.1 8.9 %multiply_convert_fusion = bf16[1024,4096]{1,0:T(8,128)(2,1)} fusion(f32[1024]{0:T(1024)S(1)} %get-tuple-element.67, bf16[1024,768]{1,0:T(8,128)(2,1)S(1)} %multiply_convert_fusion.2, bf16[1,768,4096]{2,1,0:T(8,128)(2,1)S(1)} %bitcast.120), kind=kOutput, calls=%fused_computation.22 | convolution fusion | flops 6459228160 | bytes 16257024 | tf_op jit(solution)/shard_map/dot_general | solution.py:186
  452.0 70.0 %reduce-scatter.6.cloned.1.call-done = bf16[64,4096]{1,0:T(8,128)(2,1)} async-done(((bf16[1024,4096]{1,0:T(8,128)(2,1)}), bf16[64,4096]{1,0:T(8,128)(2,1)}) %reduce-scatter.6.cloned.1.call-update) | async-done | bytes 524304 | tf_op jit(solution)/shard_map/reduce_scatter | solution.py:194
  521.9 109.0 %reduce-scatter.8.cloned.1.call-done = bf16[64,4096]{1,0:T(8,128)(2,1)} async-done(((bf16[1024,4096]{1,0:T(8,128)(2,1)}), bf16[64,4096]{1,0:T(8,128)(2,1)}) %reduce-scatter.8.cloned.1.call-update) | async-done | bytes 524304 | tf_op jit(solution)/shard_map/reduce_scatter | solution.py:194
  630.9 2.4 fusion.38
  633.4 2.5 reshape.226
  (83 shorter events, 7.1 us)
Async XLA Ops:
  6.5 5.4 copy-start
  6.5 6.5 %copy-start.4 = (bf16[1,256,2,1024]{3,2,1,0:T(2,128)(2,1)S(1)}, bf16[1,256,2,1024]{3,2,1,0:T(2,128)(2,1)}, u32[]{:S(2)}) copy-start(bf16[1,256,2,1024]{3,2,1,0:T(2,128)(2,1)} %param.15) | copy-start | bytes 3145732
  6.5 8.4 %copy-start.9 = (f32[128]{0:T(128)S(1)}, f32[128]{0:T(128)}, u32[]{:S(2)}) copy-start(f32[128]{0:T(128)} %param.18) | copy-start | bytes 1540
  6.5 36.1 %all-gather.6.cloned.1.call-start = ((), (), s32[]{:S(2)}) async-start(), calls=%async_computation.3 | async-start | bytes 1310720 | tf_op jit(solution)/shard_map/all_gather | solution.py:123
  11.8 157.4 %all-gather.12.cloned.1.call-start = ((), (), s32[]{:S(2)}) async-start(), calls=%async_computation.9 | async-start | bytes 9437184 | tf_op jit(solution)/shard_map/all_gather | solution.py:144
  13.0 220.1 %reduce-scatter.4.cloned.1.call-start = ((), (), s32[]{:S(2)}) async-start(), calls=%async_computation.4 | async-start | bytes 5242880 | tf_op jit(solution)/shard_map/reduce_scatter | solution.py:148
  43.5 8.6 %copy-start.6 = (bf16[1024,2,1,256]{3,0,1,2:T(8,128)(2,1)S(1)}, bf16[1024,2,1,256]{3,0,1,2:T(8,128)(2,1)}, u32[]{:S(2)}) copy-start(bf16[1024,2,1,256]{3,0,1,2:T(8,128)(2,1)} %get-tuple-element.25) | copy-start | bytes 3145732 | tf_op jit(solution)/shard_map/cond
  180.7 9.7 %copy-start.3 = (bf16[1,64,2,4096]{3,2,1,0:T(2,128)(2,1)S(1)}, bf16[1,64,2,4096]{3,2,1,0:T(2,128)(2,1)}, u32[]{:S(2)}) copy-start(bf16[1,64,2,4096]{3,2,1,0:T(2,128)(2,1)} %param.21) | copy-start | bytes 3145732
  190.3 44.5 %copy-start.7 = (f32[4096]{0:T(1024)S(1)}, f32[4096]{0:T(1024)}, u32[]{:S(2)}) copy-start(f32[4096]{0:T(1024)} %param.22) | copy-start | bytes 49156
  190.3 46.6 %copy-start.8 = (s32[1,64,2,8]{1,3,2,0:T(8,128)S(1)}, s32[1,64,2,8]{1,3,2,0:T(8,128)}, u32[]{:S(2)}) copy-start(s32[1,64,2,8]{1,3,2,0:T(8,128)} %param.24) | copy-start | bytes 12292
  190.3 121.8 %copy-start.5 = (bf16[4096,16]{0,1:T(8,128)(2,1)S(1)}, bf16[4096,16]{0,1:T(8,128)(2,1)}, u32[]{:S(2)}) copy-start(bf16[4096,16]{0,1:T(8,128)(2,1)} %param.23) | copy-start | bytes 393220
  190.3 121.8 %all-gather.10.cloned.1.call-start = ((), (), s32[]{:S(2)}) async-start(), calls=%async_computation.7 | async-start | bytes 8912896 | tf_op jit(solution)/shard_map/all_gather | solution.py:174
  236.2 151.4 %all-gather.8.cloned.1.call-start = ((), (), s32[]{:S(2)}) async-start(), calls=%async_computation.5 | async-start | bytes 8912896 | tf_op jit(solution)/shard_map/all_gather | solution.py:174
  236.8 285.1 %reduce-scatter.6.cloned.1.call-start = ((), (), s32[]{:S(2)}) async-start(), calls=%async_computation.6 | async-start | bytes 8912896 | tf_op jit(solution)/shard_map/reduce_scatter | solution.py:194
  387.6 6.0 copy-start.2
  387.6 15.4 %slice-start = ((s8[6291456]{0:T(1024)(128)(4,1)}), s8[4194304]{0:T(1024)(128)(4,1)S(1)}, s32[]{:S(2)}) async-start(s8[6291456]{0:T(1024)(128)(4,1)} %bitcast.115), calls=%async_computation.10 | async-start | bytes 8388608
  393.6 9.4 %slice-start.1 = ((s8[6291456]{0:T(1024)(128)(4,1)}), s8[2097152]{0:T(1024)(128)(4,1)S(1)}, s32[]{:S(2)}) async-start(s8[6291456]{0:T(1024)(128)(4,1)} %bitcast.115), calls=%async_computation.11 | async-start | bytes 4194304
  393.6 16.4 %slice-start.2 = ((s8[6291456]{0:T(1024)(128)(4,1)}), s8[4194304]{0:T(1024)(128)(4,1)S(1)}, s32[]{:S(2)}) async-start(s8[6291456]{0:T(1024)(128)(4,1)} %bitcast.117), calls=%async_computation.12 | async-start | bytes 8388608
  403.0 7.0 %slice-start.3 = ((s8[6291456]{0:T(1024)(128)(4,1)}), s8[2097152]{0:T(1024)(128)(4,1)S(1)}, s32[]{:S(2)}) async-start(s8[6291456]{0:T(1024)(128)(4,1)} %bitcast.117), calls=%async_computation.13 | async-start | bytes 4194304
  418.9 212.0 %reduce-scatter.8.cloned.1.call-start = ((), (), s32[]{:S(2)}) async-start(), calls=%async_computation.8 | async-start | bytes 8912896 | tf_op jit(solution)/shard_map/reduce_scatter | solution.py:194
  419.0 24.1 %slice-start.4 = ((s8[6291456]{0:T(1024)(128)(4,1)}), s8[4194304]{0:T(1024)(128)(4,1)S(1)}, s32[]{:S(2)}) async-start(s8[6291456]{0:T(1024)(128)(4,1)} %bitcast.119), calls=%async_computation.14 | async-start | bytes 8388608
  430.7 12.4 %slice-start.5 = ((s8[6291456]{0:T(1024)(128)(4,1)}), s8[2097152]{0:T(1024)(128)(4,1)S(1)}, s32[]{:S(2)}) async-start(s8[6291456]{0:T(1024)(128)(4,1)} %bitcast.119), calls=%async_computation.15 | async-start | bytes 4194304
  451.9 183.9 %copy-start.1 = (bf16[1024,1024]{1,0:T(8,128)(2,1)S(1)}, bf16[1024,1024]{1,0:T(8,128)(2,1)}, u32[]{:S(2)}) copy-start(bf16[1024,1024]{1,0:T(8,128)(2,1)} %param.20) | copy-start | bytes 6291460
Sparse Core Ops, SparseCore 0:
  12.0 30.6 all-gather.5
  44.7 124.4 all-gather.11
  190.4 42.7 reduce-scatter.3
  236.3 75.7 all-gather.9
  314.4 73.1 all-gather.7
  419.1 102.8 reduce-scatter.5
  526.6 104.3 reduce-scatter.7

commit v2 on v1

--- a/solution.py
+++ b/solution.py
@@ -75,6 +75,31 @@
         & (start_row + piece_len > low_bound)
     )
     return lax.cond(live_piece, compute, lambda carry_inner: carry_inner, carry_state)
+
+
+def fold_halves(total, name, dim):
+    members = total.shape[dim]
+    place = lax.axis_index(name)
+    step = 1
+    while step < members:
+        shape = total.shape
+        total = total.reshape(shape[:dim] + (shape[dim] // 2, 2) + shape[dim + 1 :])
+        bit = (place // step) % 2
+        keep = lax.dynamic_index_in_dim(total, bit, dim + 1, keepdims=False)
+        send = lax.dynamic_index_in_dim(total, 1 - bit, dim + 1, keepdims=False)
+        got = lax.ppermute(send, name, [(i, i ^ step) for i in range(members)])
+        total = (keep.astype(jnp.float32) + got.astype(jnp.float32)).astype(total.dtype)
+        step *= 2
+    return total
+
+
+def sum_to_owner(rows, tensor_count, split_count):
+    if tensor_count & (tensor_count - 1) or split_count & (split_count - 1):
+        return lax.psum_scatter(rows, ("tensor", "expert"), scatter_dimension=0, tiled=True)
+    total = rows.reshape(tensor_count, split_count, -1, rows.shape[1])
+    total = fold_halves(total, "tensor", 0)
+    total = fold_halves(total, "expert", 1)
+    return total.reshape(-1, rows.shape[1])
 
 
 def on_device(
@@ -120,17 +145,14 @@
         jnp.zeros(stat_shape + (head_dim,), jnp.float32),
     )
     own_high = place_index * block_len + block_len
-    kv_pack = lax.all_gather(
-        jnp.concatenate([k_ready, v_ready], axis=-1), "expert", axis=0, tiled=True
-    )
     folded = attend(
         fresh_state,
         q_ready,
         q_places,
         0,
         own_high,
-        kv_pack[..., :head_dim],
-        kv_pack[..., head_dim:],
+        lax.all_gather(k_ready, "expert", axis=0, tiled=True),
+        lax.all_gather(v_ready, "expert", axis=0, tiled=True),
         jnp.int32(0),
         score_scale,
     )
@@ -142,14 +164,24 @@
     share = out_weight.shape[1] // lax.axis_size("dp")
     own_share = lax.dynamic_slice_in_dim(out_weight, lax.axis_index("dp") * share, share, 1)
     weight_parts = lax.all_gather(own_share, ("expert", "dp"), axis=0, tiled=False)
-    partial_value = jnp.einsum(
-        "rc,gcn->rgn", attn_rows, weight_parts, preferred_element_type=jnp.float32
-    ).reshape(attn_rows.shape[0], -1)
+    row_count = hidden_in.shape[1] * seq_count
+    top_count = expert_ids.shape[3]
+    spread = ("tensor", "expert")
+    chosen = lax.all_gather(expert_ids.reshape(row_count, top_count), spread, axis=0)
+    attn_rows, chosen = lax.optimization_barrier((attn_rows, chosen))
+    partial_value = jnp.concatenate(
+        [
+            jnp.dot(attn_rows, weight_parts[part], preferred_element_type=jnp.float32).astype(
+                jnp.bfloat16
+            )
+            for part in range(weight_parts.shape[0])
+        ],
+        axis=1,
+    )
     mixed_rows = lax.psum_scatter(
-        partial_value.astype(jnp.bfloat16), "tensor", scatter_dimension=0, tiled=True
+        partial_value, "tensor", scatter_dimension=0, tiled=True
     ).astype(jnp.float32)
     d_model = hidden_in.shape[3]
-    row_count = hidden_in.shape[1] * seq_count
     stream = (hidden_in.reshape(row_count, d_model).astype(jnp.float32) + mixed_rows).astype(
         jnp.bfloat16
     )
@@ -162,9 +194,6 @@
     local_experts = w_gate.shape[0]
     device_count = tensor_count * split_count
     experts = local_experts * device_count
-    top_count = expert_ids.shape[3]
-    spread = ("tensor", "expert")
-    chosen = lax.all_gather(expert_ids.reshape(row_count, top_count), spread, axis=0)
     catalog = jnp.arange(experts, dtype=jnp.int32)
     first_expert = (lax.axis_index("tensor") * split_count + place_index) * local_experts
     piece_rows = row_count // chunk_count
@@ -172,6 +201,8 @@
     for chunk in range(chunk_count):
         span = slice(chunk * piece_rows, (chunk + 1) * piece_rows)
         rows = lax.all_gather(normed[span], spread, axis=0, tiled=True)
+        if chunk > 0:
+            rows, _ = lax.optimization_barrier((rows, share_sum))
         ids = chosen[:, span].reshape(-1, top_count)
         named = jnp.any(ids[:, :, None] == catalog[None, None, :], axis=1)
         logits = jnp.dot(rows, router, preferred_element_type=jnp.float32)
@@ -190,11 +221,8 @@
                 jnp.where(catalog == first_expert + local, gates, 0.0), axis=-1, keepdims=True
             )
             share_sum = share_sum + own_gate * expert_rows.astype(jnp.float32)
-        blended.append(
-            lax.psum_scatter(
-                share_sum.astype(jnp.bfloat16), spread, scatter_dimension=0, tiled=True
-            )
-        )
+        share_sum = share_sum.astype(jnp.bfloat16)
+        blended.append(sum_to_owner(share_sum, tensor_count, split_count))
     blended = jnp.concatenate(blended, axis=0).astype(jnp.float32)
     final_rows = (stream_f + blended).astype(jnp.bfloat16)
     return final_rows.reshape(hidden_in.shape)

time: 652 us -> 589 us (0.903)
  waiting for transfers between devices: 454 us -> 321 us
  blocking collectives: 32.3 us -> 78.6 us
  local copies, waits for them, and re-layouts: 19.8 us -> 31.8 us
  other arithmetic: 20.7 us -> 31.4 us
    reduce_scatter x3 -> x1, waiting for transfers between devices: 221 us -> 41.3 us  [on_device(): lax.psum_scatter(partial_value, 'tensor', scatter_dimension=0, tiled=True)]
    ppermute x0 -> x8, waiting for transfers between devices: none -> 138 us  [fold_halves(): got = lax.ppermute(send, name, [(i, i ^ step) for i in range(members)])]
    all_gather x1, waiting for transfers between devices: 93 us -> 26.1 us  [on_device(): lax.all_gather(own_share, ('expert', 'dp'), axis=0, tiled=False)]
    all_gather x0 -> x2, blocking collectives: none -> 46.1 us  [the longest x1 24 us: on_device(): lax.all_gather(k_ready, 'expert', axis=0, tiled=True)]
    all_gather x1 -> x0, waiting for transfers between devices: 26.9 us -> none  [on_device(): lax.all_gather(jnp.concatenate([k_ready, v_ready], axis=-1), 'expert', ax...]
    unnamed x33 -> x55, local copies, waits for them, and re-layouts: 2.16 us -> 16.6 us
    convert_element_type x0 -> x6, other arithmetic: none -> 14.1 us  [fold_halves(): (keep.astype(jnp.float32) + got.astype(jnp.float32)).astype(total.dtype)]
    dot_general x1 -> x0, local copies, waits for them, and re-layouts: 11.5 us -> none  [on_device(): jnp.einsum('rc,gcn->rgn', attn_rows, weight_parts, preferred_element_type...]
  transfers between devices with their start and end apart: 7 -> 12, of which waited for: 7 -> 8; matrix products, arithmetic and copies ran while one was open for 12% -> 21% of each run, Pallas kernels for 0% -> 0%
where the time goes in v2:
time: 589 us; the launch traced here: 580 us
  waiting for transfers between devices  321 us (54%)
  matrix products  96.8 us (16%)
  blocking collectives  78.6 us (13%)
  local copies, waits for them, and re-layouts  31.8 us (5%)
  other arithmetic  31.4 us (5%)
  between operations  14.9 us (3%)
  starting transfers between devices  5.96 us (1%)
    ppermute x8, waiting for transfers between devices, fold_halves(): got = lax.ppermute(send, name, [(i, i ^ step) for i in range(members)])  138 us
    all_gather x2, waiting for transfers between devices, on_device(): rows = lax.all_gather(normed[span], spread, axis=0, tiled=True)  115 us
    reduce_scatter x1, waiting for transfers between devices, on_device(): lax.psum_scatter(partial_value, 'tensor', scatter_dimension=0, tiled=True)  41.3 us
    all_gather x1, blocking collectives, on_device(): lax.all_gather(expert_ids.reshape(row_count, top_count), spread, axis=0)  32.5 us
    all_gather x1, waiting for transfers between devices, on_device(): lax.all_gather(own_share, ('expert', 'dp'), axis=0, tiled=False)  26.1 us
    all_gather x1, blocking collectives, on_device(): lax.all_gather(k_ready, 'expert', axis=0, tiled=True)  24 us
    all_gather x1, blocking collectives, on_device(): lax.all_gather(v_ready, 'expert', axis=0, tiled=True)  22.1 us
    dot_general x2, matrix products, on_device(): up_part = jnp.dot(rows, w_up[local], preferred_element_type=jnp.float32)  20.7 us
  transfers between devices with their start and end apart: 12, of which 8 were waited for; matrix products, arithmetic and copies ran while one was open for 21% of the time, Pallas kernels for 0%

profile of v2, /device:TPU:0, one launch (start us, length us, event | category | flops | bytes accessed | tf_op | source)
XLA Modules:
  0.0 580.3 jit_solution(10283087723534186599)
XLA Ops:
  9.3 2.4 copy.74
  15.2 24.0 %all_gather.21 = bf16[1024,2,1,128]{3,0,1,2:T(8,128)(2,1)S(1)} all-gather(bf16[256,2,1,128]{3,0,1,2:T(8,128)(2,1)S(1)} %pad_maximum_fusion.1), channel_id=1, replica_groups=mesh['tensor'=4,'expert'=4,'dp'=2] {'expert'}, dimensions={0}, use_global_device_ids=true | all-gather | bytes 655360 | tf_op jit(solution)/shard_map/all_gather | solution.py:154
  39.2 22.1 %all-gather = bf16[1,1024,2,128]{3,1,2,0:T(8,128)(2,1)S(1)} all-gather(bf16[1,256,2,128]{3,1,2,0:T(8,128)(2,1)S(1)} %copy.75), channel_id=2, replica_groups=mesh['tensor'=4,'expert'=4,'dp'=2] {'expert'}, dimensions={1}, use_global_device_ids=true | all-gather | bytes 655360 | tf_op jit(solution)/shard_map/all_gather | solution.py:155
  61.3 29.2 %conditional.1 = (f32[2,1,8,256]{3,2,0,1:T(8,128)S(1)}, f32[2,1,8,256,128]{4,3,2,0,1:T(8,128)}) conditional(s32[]{:T(128)} %convert_element_type.244, () %tuple.15, (s32[1024]{0:T(1024)S(1)}, s32[256]{0:T(256)S(1)}, s32[1024]{0:T(1024)S(1)}, s32[]{:T(128)}, s32[1024]{0:T(1024)S(1)}, /*index=5*/bf16[1024,2,1,128]{3,0,1,2:T(8,128)(2,1)S(1)}, ...), branch_computations={%region_3.0_spmd, %region_4.7_spmd} | conditional | flops 2202793984 | bytes 55690260 | solution.py:77
  62.2 7.1 %fusion = (f32[2,8,256]{2,1,0:T(8,128)S(1)}, f32[2,1024,256,8]{2,1,3,0:T(8,128)}) fusion(pred[256,1024]{0,1:T(8,128)(4,1)S(1)} %and_and_fusion, bf16[256,2,1,8,128]{0,4,3,1,2:T(8,128)(2,1)S(1)} %get-tuple-element.67, bf16[1024,2,1,128]{3,0,1,2:T(8,128)(2,1)S(1)} %get-tuple-element.24), kind=kOutput, calls=%fused_computation.2 | convolution fusion | flops 1086320640 | bytes 18628608 | tf_op jit(solution)/shard_map/cond/branch_1_fun/pskgd,nskd->skgpn/dot_general | solution.py:50
  69.4 12.7 %fusion.7 = f32[2,1,8,256,128]{4,3,2,0,1:T(8,128)} fusion(f32[2,1024,256,8]{2,1,3,0:T(8,128)} %get-tuple-element.72, f32[2,8,256]{2,1,0:T(8,128)S(1)} %broadcast_maximum_fusion, pred[256,1024]{0,1:T(8,128)(4,1)S(1)} %and_and_fusion, bf16[1024,2,1,128]{3,0,1,2:T(8,128)(2,1)S(1)} %get-tuple-element.26), kind=kOutput, calls=%fused_computation.8 | convolution fusion | flops 1094713344 | bytes 19677184 | tf_op jit(solution)/shard_map/cond/branch_1_fun/skgpn,nskd->skgpd/dot_general | solution.py:64
  82.0 8.0 %fusion.2 = f32[2,8,256]{2,1,0:T(8,128)S(1)} fusion(f32[2,1024,256,8]{2,1,3,0:T(8,128)} %get-tuple-element.72, f32[2,8,256]{2,1,0:T(8,128)S(1)} %broadcast_maximum_fusion, pred[256,1024]{0,1:T(8,128)(4,1)S(1)} %and_and_fusion), kind=kLoop, calls=%fused_computation.4 | loop fusion | flops 20967424 | bytes 17072128 | tf_op jit(solution)/shard_map/cond/branch_1_fun/reduce_sum | solution.py:63
  93.6 32.5 %all_gather.23 = s32[16,128,8]{1,2,0:T(8,128)S(1)} all-gather(s32[1,128,8]{1,2,0:T(8,128)S(1)} %copy.79), channel_id=1, replica_groups=mesh['tensor'=4,'expert'=4,'dp'=2] {'tensor','expert'}, dimensions={0}, use_global_device_ids=true | all-gather | bytes 69632 | tf_op jit(solution)/shard_map/all_gather | solution.py:170
  126.1 26.1 %all-gather.10.cloned.1.call-done = bf16[8192,512]{1,0:T(8,128)(2,1)} async-done(((bf16[1024,512]{1,0:T(8,128)(2,1)}), bf16[8192,512]{1,0:T(8,128)(2,1)}) %all-gather.10.cloned.1.call-update) | async-done | bytes 8388624 | tf_op jit(solution)/shard_map/all_gather | solution.py:166
  152.2 2.9 fusion.48
  155.1 2.8 fusion.47
  157.9 2.8 fusion.46
  168.6 6.4 %copy.90 = bf16[512,4096]{1,0:T(8,128)(2,1)} copy(bf16[512,4096]{0,1:T(8,128)(2,1)} %fusion.41) | data formatting | bytes 8388608
  176.6 41.3 %reduce-scatter.4.cloned.1.call-done = bf16[128,4096]{1,0:T(8,128)(2,1)} async-done(((bf16[512,4096]{1,0:T(8,128)(2,1)}), bf16[128,4096]{1,0:T(8,128)(2,1)}) %reduce-scatter.4.cloned.1.call-update) | async-done | bytes 1048592 | tf_op jit(solution)/shard_map/reduce_scatter | solution.py:181
  222.0 74.0 %all-gather.6.cloned.1.call-done = bf16[1024,4096]{1,0:T(8,128)(2,1)} async-done(((bf16[64,4096]{1,0:T(8,128)(2,1)}), bf16[1024,4096]{1,0:T(8,128)(2,1)}) %all-gather.6.cloned.1.call-update) | async-done | bytes 8388624 | tf_op jit(solution)/shard_map/all_gather | solution.py:203
  296.0 5.8 %select_reduce_fusion.3 = (f32[1024]{0:T(1024)S(1)}, f32[1024,16]{0,1:T(8,128)S(1)}) fusion(pred[1024,16]{0,1:T(8,128)(4,1)S(1)} %fusion.62, bf16[1024,4096]{1,0:T(8,128)(2,1)} %all-gather.6.cloned.1.call-done, bf16[4096,16]{0,1:T(8,128)(2,1)S(1)} %copy-done.11), kind=kOutput, calls=%fused_computation.114 | convolution fusion | flops 134249472 | bytes 8605696 | tf_op jit(solution)/shard_map/dot_general | solution.py:208
  302.0 9.4 %fusion.23 = f32[1024,768]{1,0:T(8,128)S(1)} fusion(bf16[1024,4096]{1,0:T(8,128)(2,1)S(1)} %copy-done.6, bf16[1,4096,768]{2,1,0:T(8,128)(2,1)} %param.26), kind=kOutput, calls=%fused_computation.30 | convolution fusion | flops 6442450944 | bytes 17825792 | tf_op jit(solution)/shard_map/dot_general | solution.py:215
  311.5 7.0 %multiply_convert_fusion.3 = bf16[1024,768]{1,0:T(8,128)(2,1)S(1)} fusion(f32[1024,768]{1,0:T(8,128)S(1)} %fusion.23, bf16[1024,4096]{1,0:T(8,128)(2,1)S(1)} %copy-done.6, bf16[1,4096,768]{2,1,0:T(8,128)(2,1)S(1)} %bitcast.168), kind=kOutput, calls=%fused_computation.41 | convolution fusion | flops 6447169536 | bytes 19398656 | tf_op jit(solution)/shard_map/dot_general | solution.py:214
  318.5 7.3 %multiply_convert_fusion.1 = bf16[1024,4096]{1,0:T(8,128)(2,1)S(1)} fusion(f32[1024]{0:T(1024)S(1)} %select_reduce_fusion.2, bf16[1024,768]{1,0:T(8,128)(2,1)S(1)} %multiply_convert_fusion.3, bf16[1,768,4096]{2,1,0:T(8,128)(2,1)S(1)} %bitcast.170), kind=kOutput, calls=%fused_computation.21 | convolution fusion | flops 6459228160 | bytes 16257024 | tf_op jit(solution)/shard_map/dot_general | solution.py:217
  325.8 2.8 dynamic-slice_bitcast_fusion.1
  330.6 40.9 %all-gather.8.cloned.1.call-done = bf16[1024,4096]{1,0:T(8,128)(2,1)} async-done(((bf16[64,4096]{1,0:T(8,128)(2,1)}), bf16[1024,4096]{1,0:T(8,128)(2,1)}) %all-gather.8.cloned.1.call-update) | async-done | bytes 8388624 | tf_op jit(solution)/shard_map/all_gather | solution.py:203
  371.5 11.2 %fusion.21 = f32[1024,768]{1,0:T(8,128)S(1)} fusion(bf16[1024,4096]{1,0:T(8,128)(2,1)} %all-gather.8.cloned.1.call-done, bf16[1,4096,768]{2,1,0:T(8,128)(2,1)} %param.26), kind=kOutput, calls=%fused_computation.28 | convolution fusion | flops 6442450944 | bytes 17825792 | tf_op jit(solution)/shard_map/dot_general | solution.py:215
  382.8 9.9 %multiply_convert_fusion.2 = bf16[1024,768]{1,0:T(8,128)(2,1)S(1)} fusion(f32[1024,768]{1,0:T(8,128)S(1)} %fusion.21, bf16[1024,4096]{1,0:T(8,128)(2,1)S(1)} %copy-done.5, bf16[1,4096,768]{2,1,0:T(8,128)(2,1)} %param.25), kind=kOutput, calls=%fused_computation.40 | convolution fusion | flops 6447169536 | bytes 19398656 | tf_op jit(solution)/shard_map/dot_general | solution.py:214
  395.2 7.6 %multiply_convert_fusion = bf16[1024,4096]{1,0:T(8,128)(2,1)S(1)} fusion(f32[1024]{0:T(1024)S(1)} %select_reduce_fusion, bf16[1024,768]{1,0:T(8,128)(2,1)S(1)} %multiply_convert_fusion.2, bf16[1,768,4096]{2,1,0:T(8,128)(2,1)S(1)} %bitcast.172), kind=kOutput, calls=%fused_computation.20 | convolution fusion | flops 6459228160 | bytes 16257024 | tf_op jit(solution)/shard_map/dot_general | solution.py:217
  402.8 2.8 dynamic-slice_bitcast_fusion
  407.5 5.2 fusion.18
  414.9 3.7 fusion.17
  422.8 40.2 %collective-permute-done.1 = bf16[1,4,64,4096]{3,2,1,0:T(8,128)(2,1)S(1)} collective-permute-done((bf16[1,4,64,4096]{3,2,1,0:T(8,128)(2,1)}, bf16[1,4,64,4096]{3,2,1,0:T(8,128)(2,1)S(1)}, u32[]{:S(2)}, u32[]{:S(2)}) %collective-permute-start.1) | collective-permute-done | bytes 2097184 | tf_op jit(solution)/shard_map/ppermute | solution.py:90
  466.4 40.9 %collective-permute-done.5 = bf16[1,4,64,4096]{3,2,1,0:T(8,128)(2,1)} collective-permute-done((bf16[1,4,64,4096]{3,2,1,0:T(8,128)(2,1)}, bf16[1,4,64,4096]{3,2,1,0:T(8,128)(2,1)}, u32[]{:S(2)}, u32[]{:S(2)}) %collective-permute-start.5) | collective-permute-done | bytes 2097184 | tf_op jit(solution)/shard_map/ppermute | solution.py:90
  512.4 33.2 %collective-permute-done.6 = bf16[1,2,64,4096]{3,2,1,0:T(8,128)(2,1)S(1)} collective-permute-done((bf16[1,2,64,4096]{3,2,1,0:T(8,128)(2,1)S(1)}, bf16[1,2,64,4096]{3,2,1,0:T(8,128)(2,1)S(1)}, u32[]{:S(2)}, u32[]{:S(2)}) %collective-permute-start.6) | collective-permute-done | bytes 1048608 | tf_op jit(solution)/shard_map/ppermute | solution.py:90
  546.2 23.3 %collective-permute-done.7 = bf16[1,1,64,4096]{3,2,1,0:T(8,128)(2,1)S(1)} collective-permute-done((bf16[1,1,64,4096]{3,2,1,0:T(8,128)(2,1)S(1)}, bf16[1,1,64,4096]{3,2,1,0:T(8,128)(2,1)S(1)}, u32[]{:S(2)}, u32[]{:S(2)}) %collective-permute-start.7) | collective-permute-done | bytes 524320 | tf_op jit(solution)/shard_map/ppermute | solution.py:90
  570.8 2.5 reshape.300
  (136 shorter events, 46.1 us)
Async XLA Ops:
  6.5 6.4 %copy-start.13 = (bf16[1,256,2,128]{3,2,1,0:T(2,128)(2,1)S(1)}, bf16[1,256,2,128]{3,2,1,0:T(2,128)(2,1)}, u32[]{:S(2)}) copy-start(bf16[1,256,2,128]{3,2,1,0:T(2,128)(2,1)} %param.17) | copy-start | bytes 393220
  6.5 7.1 %copy-start.12 = (bf16[1,256,2,128]{3,2,1,0:T(2,128)(2,1)S(1)}, bf16[1,256,2,128]{3,2,1,0:T(2,128)(2,1)}, u32[]{:S(2)}) copy-start(bf16[1,256,2,128]{3,2,1,0:T(2,128)(2,1)} %param.16) | copy-start | bytes 393220
  6.5 7.2 %copy-start.16 = (f32[128]{0:T(128)S(1)}, f32[128]{0:T(128)}, u32[]{:S(2)}) copy-start(f32[128]{0:T(128)} %param.19) | copy-start | bytes 1540
  6.5 145.7 %all-gather.10.cloned.1.call-start = ((), (), s32[]{:S(2)}) async-start(), calls=%async_computation.3 | async-start | bytes 9437184 | tf_op jit(solution)/shard_map/all_gather | solution.py:166
  8.1 6.3 %copy-start.17 = (f32[128]{0:T(128)S(1)}, f32[128]{0:T(128)}, u32[]{:S(2)}) copy-start(f32[128]{0:T(128)} %param.18) | copy-start | bytes 1540
  9.2 208.7 %reduce-scatter.4.cloned.1.call-start = ((), (), s32[]{:S(2)}) async-start(), calls=%async_computation.4 | async-start | bytes 5242880 | tf_op jit(solution)/shard_map/reduce_scatter | solution.py:181
  152.2 8.5 %copy-start.18 = (bf16[8192,512]{1,0:T(8,128)(2,1)S(1)}, bf16[8192,512]{1,0:T(8,128)(2,1)}, u32[]{:S(2)}) copy-start(bf16[8192,512]{1,0:T(8,128)(2,1)} %all-gather.10.cloned.1.call-done) | copy-start | bytes 25165828
  175.0 44.5 %copy-start.14 = (f32[4096]{0:T(1024)S(1)}, f32[4096]{0:T(1024)}, u32[]{:S(2)}) copy-start(f32[4096]{0:T(1024)} %param.22) | copy-start | bytes 49156
  175.1 121.0 %all-gather.6.cloned.1.call-start = ((), (), s32[]{:S(2)}) async-start(), calls=%async_computation.1 | async-start | bytes 8912896 | tf_op jit(solution)/shard_map/all_gather | solution.py:203
  176.6 119.4 %copy-start.11 = (bf16[4096,16]{0,1:T(8,128)(2,1)S(1)}, bf16[4096,16]{0,1:T(8,128)(2,1)}, u32[]{:S(2)}) copy-start(bf16[4096,16]{0,1:T(8,128)(2,1)} %param.23) | copy-start | bytes 393220
  221.0 150.5 %all-gather.8.cloned.1.call-start = ((), (), s32[]{:S(2)}) async-start(), calls=%async_computation.2 | async-start | bytes 8912896 | tf_op jit(solution)/shard_map/all_gather | solution.py:203
  296.0 6.0 %copy-start.6 = (bf16[1024,4096]{1,0:T(8,128)(2,1)S(1)}, bf16[1024,4096]{1,0:T(8,128)(2,1)}, u32[]{:S(2)}) copy-start(bf16[1024,4096]{1,0:T(8,128)(2,1)} %all-gather.6.cloned.1.call-done) | copy-start | bytes 25165828
  296.0 15.4 %slice-start = ((s8[6291456]{0:T(1024)(128)(4,1)}), s8[4194304]{0:T(1024)(128)(4,1)S(1)}, s32[]{:S(2)}) async-start(s8[6291456]{0:T(1024)(128)(4,1)} %bitcast.167), calls=%async_computation.5 | async-start | bytes 8388608
  302.0 9.5 %slice-start.1 = ((s8[6291456]{0:T(1024)(128)(4,1)}), s8[2097152]{0:T(1024)(128)(4,1)S(1)}, s32[]{:S(2)}) async-start(s8[6291456]{0:T(1024)(128)(4,1)} %bitcast.167), calls=%async_computation.6 | async-start | bytes 4194304
  302.0 16.5 %slice-start.2 = ((s8[6291456]{0:T(1024)(128)(4,1)}), s8[4194304]{0:T(1024)(128)(4,1)S(1)}, s32[]{:S(2)}) async-start(s8[6291456]{0:T(1024)(128)(4,1)} %bitcast.169), calls=%async_computation.7 | async-start | bytes 8388608
  311.5 7.0 %slice-start.3 = ((s8[6291456]{0:T(1024)(128)(4,1)}), s8[2097152]{0:T(1024)(128)(4,1)S(1)}, s32[]{:S(2)}) async-start(s8[6291456]{0:T(1024)(128)(4,1)} %bitcast.169), calls=%async_computation.8 | async-start | bytes 4194304
  325.8 4.6 copy-start.7
  330.4 77.2 %collective-permute-start = (bf16[2,4,64,4096]{3,2,1,0:T(8,128)(2,1)}, bf16[2,4,64,4096]{3,2,1,0:T(8,128)(2,1)}, u32[]{:S(2)}, u32[]{:S(2)}) collective-permute-start(bf16[2,4,64,4096]{3,2,1,0:T(8,128)(2,1)} %dynamic-slice_bitcast_fusion.1), channel_id=1, source_target_pairs={{0,8},{8,0},{16,24},{24,16},{1,9},{9,1},{17,25},{25,17},{2,10},{10... | collective-permute-start | bytes 12582920 | tf_op jit(solution)/shard_map/ppermute | solution.py:90
  371.5 11.3 %copy-start.5 = (bf16[1024,4096]{1,0:T(8,128)(2,1)S(1)}, bf16[1024,4096]{1,0:T(8,128)(2,1)}, u32[]{:S(2)}) copy-start(bf16[1024,4096]{1,0:T(8,128)(2,1)} %all-gather.8.cloned.1.call-done) | copy-start | bytes 25165828
  371.5 23.6 %slice-start.4 = ((s8[6291456]{0:T(1024)(128)(4,1)}), s8[4194304]{0:T(1024)(128)(4,1)S(1)}, s32[]{:S(2)}) async-start(s8[6291456]{0:T(1024)(128)(4,1)} %bitcast.171), calls=%async_computation.9 | async-start | bytes 8388608
  382.8 12.4 %slice-start.5 = ((s8[6291456]{0:T(1024)(128)(4,1)}), s8[2097152]{0:T(1024)(128)(4,1)S(1)}, s32[]{:S(2)}) async-start(s8[6291456]{0:T(1024)(128)(4,1)} %bitcast.171), calls=%async_computation.10 | async-start | bytes 4194304
  407.3 7.6 %collective-permute-start.4 = (bf16[2,4,64,4096]{3,2,1,0:T(8,128)(2,1)}, bf16[2,4,64,4096]{3,2,1,0:T(8,128)(2,1)}, u32[]{:S(2)}, u32[]{:S(2)}) collective-permute-start(bf16[2,4,64,4096]{3,2,1,0:T(8,128)(2,1)} %dynamic-slice_bitcast_fusion), channel_id=1, source_target_pairs={{0,8},{8,0},{16,24},{24,16},{1,9},{9,1},{17,25},{25,17},{2,10},{10... | collective-permute-start | bytes 12582920 | tf_op jit(solution)/shard_map/ppermute | solution.py:90
  407.5 7.4 %copy-start.9 = (bf16[1024,4096]{1,0:T(8,128)(2,1)S(1)}, bf16[1024,4096]{1,0:T(8,128)(2,1)}, u32[]{:S(2)}) copy-start(bf16[1024,4096]{1,0:T(8,128)(2,1)} %copy-done.8) | copy-start | bytes 25165828
  412.7 5.9 %copy-start.2 = (bf16[2,4,64,4096]{3,2,1,0:T(8,128)(2,1)}, bf16[2,4,64,4096]{3,2,1,0:T(8,128)(2,1)S(1)}, u32[]{:S(2)}) copy-start(bf16[2,4,64,4096]{3,2,1,0:T(8,128)(2,1)S(1)} %fusion.18) | copy-start | bytes 12582916
  414.3 48.7 %collective-permute-start.1 = (bf16[1,4,64,4096]{3,2,1,0:T(8,128)(2,1)}, bf16[1,4,64,4096]{3,2,1,0:T(8,128)(2,1)S(1)}, u32[]{:S(2)}, u32[]{:S(2)}) collective-permute-start(bf16[1,4,64,4096]{3,2,1,0:T(8,128)(2,1)} %constant_dynamic-slice_fusion.3), channel_id=1, source_target_pairs={{0,16},{8,24},{16,0},{24,8},{1,17},{9,25},{17,1},{25,9},{2,18},{10... | collective-permute-start | bytes 6291464 | tf_op jit(solution)/shard_map/ppermute | solution.py:90
  421.3 86.1 %collective-permute-start.5 = (bf16[1,4,64,4096]{3,2,1,0:T(8,128)(2,1)}, bf16[1,4,64,4096]{3,2,1,0:T(8,128)(2,1)}, u32[]{:S(2)}, u32[]{:S(2)}) collective-permute-start(bf16[1,4,64,4096]{3,2,1,0:T(8,128)(2,1)} %constant_dynamic-slice_fusion.1), channel_id=1, source_target_pairs={{0,16},{8,24},{16,0},{24,8},{1,17},{9,25},{17,1},{25,9},{2,18},{10... | collective-permute-start | bytes 6291464 | tf_op jit(solution)/shard_map/ppermute | solution.py:90
  422.8 84.6 %copy-start.4 = (bf16[2,4,64,4096]{3,2,1,0:T(8,128)(2,1)S(1)}, bf16[2,4,64,4096]{3,2,1,0:T(8,128)(2,1)}, u32[]{:S(2)}) copy-start(bf16[2,4,64,4096]{3,2,1,0:T(8,128)(2,1)} %copy-done.3) | copy-start | bytes 12582916
  465.5 45.3 %collective-permute-start.2 = (bf16[1,2,64,4096]{3,2,1,0:T(8,128)(2,1)S(1)}, bf16[1,2,64,4096]{3,2,1,0:T(8,128)(2,1)S(1)}, u32[]{:S(2)}, u32[]{:S(2)}) collective-permute-start(bf16[1,2,64,4096]{3,2,1,0:T(8,128)(2,1)S(1)} %dynamic-slice_bitcast_fusion.3), channel_id=1, source_target_pairs={{0,2},{2,0},{4,6},{6,4},{1,3},{3,1},{5,7},{7,5},{8,10},{10,8},{12,... | collective-permute-start | bytes 3145736 | tf_op jit(solution)/shard_map/ppermute | solution.py:90
  509.8 35.8 %collective-permute-start.6 = (bf16[1,2,64,4096]{3,2,1,0:T(8,128)(2,1)S(1)}, bf16[1,2,64,4096]{3,2,1,0:T(8,128)(2,1)S(1)}, u32[]{:S(2)}, u32[]{:S(2)}) collective-permute-start(bf16[1,2,64,4096]{3,2,1,0:T(8,128)(2,1)S(1)} %dynamic-slice_bitcast_fusion.2), channel_id=1, source_target_pairs={{0,2},{2,0},{4,6},{6,4},{1,3},{3,1},{5,7},{7,5},{8,10},{10,8},{12,... | collective-permute-start | bytes 3145736 | tf_op jit(solution)/shard_map/ppermute | solution.py:90
  511.1 35.0 %collective-permute-start.3 = (bf16[1,1,64,4096]{3,2,1,0:T(8,128)(2,1)S(1)}, bf16[1,1,64,4096]{3,2,1,0:T(8,128)(2,1)S(1)}, u32[]{:S(2)}, u32[]{:S(2)}) collective-permute-start(bf16[1,1,64,4096]{3,2,1,0:T(8,128)(2,1)S(1)} %constant_dynamic-slice_fusion.2), channel_id=1, source_target_pairs={{0,4},{2,6},{4,0},{6,2},{1,5},{3,7},{5,1},{7,3},{8,12},{10,14},{12... | collective-permute-start | bytes 1572872 | tf_op jit(solution)/shard_map/ppermute | solution.py:90
  545.9 27.5 %copy-start.1 = (bf16[1024,1024]{1,0:T(8,128)(2,1)S(1)}, bf16[1024,1024]{1,0:T(8,128)(2,1)}, u32[]{:S(2)}) copy-start(bf16[1024,1024]{1,0:T(8,128)(2,1)} %param.20) | copy-start | bytes 6291460
  546.0 23.5 %collective-permute-start.7 = (bf16[1,1,64,4096]{3,2,1,0:T(8,128)(2,1)S(1)}, bf16[1,1,64,4096]{3,2,1,0:T(8,128)(2,1)S(1)}, u32[]{:S(2)}, u32[]{:S(2)}) collective-permute-start(bf16[1,1,64,4096]{3,2,1,0:T(8,128)(2,1)S(1)} %constant_dynamic-slice_fusion), channel_id=1, source_target_pairs={{0,4},{2,6},{4,0},{6,2},{1,5},{3,7},{5,1},{7,3},{8,12},{10,14},{12... | collective-permute-start | bytes 1572872 | tf_op jit(solution)/shard_map/ppermute | solution.py:90
  (5 other events, 12.9 us)
Sparse Core Ops, SparseCore 0:
  9.5 142.6 all-gather.9
  175.2 42.7 reduce-scatter.3
  221.1 74.8 all-gather.5
  298.3 73.1 all-gather.7

commit v3 on v2

--- a/solution.py
+++ b/solution.py
@@ -6,7 +6,7 @@
 theta_base = 1000000.0
 eps_norm = 1e-06
 neg_fill = -1e30
-chunk_count = 2
+chunk_plan = ((0, 2, True), (2, 1, True), (3, 1, False))
 
 
 def head_norm(values_in, gain_vec):
@@ -77,29 +77,31 @@
     return lax.cond(live_piece, compute, lambda carry_inner: carry_inner, carry_state)
 
 
-def fold_halves(total, name, dim):
-    members = total.shape[dim]
+def fold_half(total, name, dim, step):
     place = lax.axis_index(name)
-    step = 1
-    while step < members:
-        shape = total.shape
-        total = total.reshape(shape[:dim] + (shape[dim] // 2, 2) + shape[dim + 1 :])
-        bit = (place // step) % 2
-        keep = lax.dynamic_index_in_dim(total, bit, dim + 1, keepdims=False)
-        send = lax.dynamic_index_in_dim(total, 1 - bit, dim + 1, keepdims=False)
-        got = lax.ppermute(send, name, [(i, i ^ step) for i in range(members)])
-        total = (keep.astype(jnp.float32) + got.astype(jnp.float32)).astype(total.dtype)
-        step *= 2
-    return total
+    shape = total.shape
+    total = total.reshape(shape[:dim] + (shape[dim] // 2, 2) + shape[dim + 1 :])
+    bit = (place // step) % 2
+    keep = lax.dynamic_index_in_dim(total, bit, dim + 1, keepdims=False)
+    send = lax.dynamic_index_in_dim(total, 1 - bit, dim + 1, keepdims=False)
+    pairs = [(i, i ^ step) for i in range(lax.axis_size(name))]
+    got = lax.ppermute(send, name, pairs)
+    return (keep.astype(jnp.float32) + got.astype(jnp.float32)).astype(total.dtype)
 
 
 def sum_to_owner(rows, tensor_count, split_count):
     if tensor_count & (tensor_count - 1) or split_count & (split_count - 1):
-        return lax.psum_scatter(rows, ("tensor", "expert"), scatter_dimension=0, tiled=True)
+        done = lax.psum_scatter(rows, ("tensor", "expert"), scatter_dimension=0, tiled=True)
+        return rows, rows, done
     total = rows.reshape(tensor_count, split_count, -1, rows.shape[1])
-    total = fold_halves(total, "tensor", 0)
-    total = fold_halves(total, "expert", 1)
-    return total.reshape(-1, rows.shape[1])
+    near = total
+    for level in range(tensor_count.bit_length() - 1):
+        total = fold_half(total, "tensor", 0, 1 << level)
+        near = total if level == 0 else near
+    middle = total
+    for level in range(split_count.bit_length() - 1):
+        total = fold_half(total, "expert", 1, 1 << level)
+    return near, middle, total.reshape(-1, rows.shape[1])
 
 
 def on_device(
@@ -196,13 +198,17 @@
     experts = local_experts * device_count
     catalog = jnp.arange(experts, dtype=jnp.int32)
     first_expert = (lax.axis_index("tensor") * split_count + place_index) * local_experts
-    piece_rows = row_count // chunk_count
+    piece_rows = row_count // 4
     blended = []
-    for chunk in range(chunk_count):
-        span = slice(chunk * piece_rows, (chunk + 1) * piece_rows)
-        rows = lax.all_gather(normed[span], spread, axis=0, tiled=True)
+    for chunk, (begin, pieces, fetch) in enumerate(chunk_plan):
+        span = slice(begin * piece_rows, (begin + pieces) * piece_rows)
+        if fetch:
+            wide = slice(begin * piece_rows, (begin + 2) * piece_rows)
+            gathered = lax.all_gather(normed[wide], spread, axis=0)
+        inside = (begin % 2) * piece_rows
+        rows = gathered[:, inside : inside + pieces * piece_rows].reshape(-1, d_model)
         if chunk > 0:
-            rows, _ = lax.optimization_barrier((rows, share_sum))
+            rows, _ = lax.optimization_barrier((rows, middle if fetch else near))
         ids = chosen[:, span].reshape(-1, top_count)
         named = jnp.any(ids[:, :, None] == catalog[None, None, :], axis=1)
         logits = jnp.dot(rows, router, preferred_element_type=jnp.float32)
@@ -214,6 +220,8 @@
             gate_part = jnp.dot(rows, w_gate[local], preferred_element_type=jnp.float32)
             up_part = jnp.dot(rows, w_up[local], preferred_element_type=jnp.float32)
             inner_act = (jax.nn.silu(gate_part) * up_part).astype(jnp.bfloat16)
+            if chunk > 0 and local == 0:
+                inner_act, _ = lax.optimization_barrier((inner_act, middle))
             expert_rows = jnp.dot(
                 inner_act, w_down[local], preferred_element_type=jnp.float32
             ).astype(jnp.bfloat16)
@@ -222,7 +230,8 @@
             )
             share_sum = share_sum + own_gate * expert_rows.astype(jnp.float32)
         share_sum = share_sum.astype(jnp.bfloat16)
-        blended.append(sum_to_owner(share_sum, tensor_count, split_count))
+        near, middle, done = sum_to_owner(share_sum, tensor_count, split_count)
+        blended.append(done)
     blended = jnp.concatenate(blended, axis=0).astype(jnp.float32)
     final_rows = (stream_f + blended).astype(jnp.bfloat16)
     return final_rows.reshape(hidden_in.shape)

time: 589 us -> 554 us (0.941)
  waiting for transfers between devices: 321 us -> 272 us
  local copies, waits for them, and re-layouts: 31.8 us -> 39.1 us
  starting transfers between devices: 5.96 us -> 12.6 us
    ppermute x8 -> x12, waiting for transfers between devices: 138 us -> 102 us  [fold_half(): got = lax.ppermute(send, name, pairs)]
    all_gather x2, waiting for transfers between devices: 115 us -> 102 us  [on_device(): gathered = lax.all_gather(normed[wide], spread, axis=0)]
    ppermute x8 -> x12, starting transfers between devices: 5.8 us -> 12.5 us  [fold_half(): got = lax.ppermute(send, name, pairs)]
    dot_general x2 -> x3, matrix products: 20.7 us -> 16.4 us  [on_device(): up_part = jnp.dot(rows, w_up[local], preferred_element_type=jnp.float32)]
    unnamed x55 -> x69, local copies, waits for them, and re-layouts: 16.6 us -> 19.4 us
    convert_element_type x6 -> x9, other arithmetic: 14.1 us -> 16.5 us  [fold_half(): (keep.astype(jnp.float32) + got.astype(jnp.float32)).astype(total.dtype)]
    dot_general x2 -> x3, matrix products: 16.9 us -> 18.6 us  [on_device(): gate_part = jnp.dot(rows, w_gate[local], preferred_element_type=jnp.float32)]
    dot_general x2 -> x3, matrix products: 14.8 us -> 14.6 us  [on_device(): jnp.dot(inner_act, w_down[local], preferred_element_type=jnp.float32)]
  transfers between devices with their start and end apart: 12 -> 16, of which waited for: 8 -> 14; matrix products, arithmetic and copies ran while one was open for 21% -> 20% of each run, Pallas kernels for 0% -> 0%
where the time goes in v3:
time: 554 us; the launch traced here: 545 us
  waiting for transfers between devices  272 us (49%)
  matrix products  94 us (17%)
  blocking collectives  78.6 us (14%)
  local copies, waits for them, and re-layouts  39.1 us (7%)
  other arithmetic  33.8 us (6%)
  between operations  15 us (3%)
  starting transfers between devices  12.6 us (2%)
    all_gather x2, waiting for transfers between devices, on_device(): gathered = lax.all_gather(normed[wide], spread, axis=0)  102 us
    ppermute x12, waiting for transfers between devices, fold_half(): got = lax.ppermute(send, name, pairs)  102 us
    reduce_scatter x1, waiting for transfers between devices, on_device(): lax.psum_scatter(partial_value, 'tensor', scatter_dimension=0, tiled=True)  41.3 us
    all_gather x1, blocking collectives, on_device(): lax.all_gather(expert_ids.reshape(row_count, top_count), spread, axis=0)  32.5 us
    all_gather x1, waiting for transfers between devices, on_device(): lax.all_gather(own_share, ('expert', 'dp'), axis=0, tiled=False)  26.1 us
    all_gather x1, blocking collectives, on_device(): lax.all_gather(k_ready, 'expert', axis=0, tiled=True)  24 us
    all_gather x1, blocking collectives, on_device(): lax.all_gather(v_ready, 'expert', axis=0, tiled=True)  22.1 us
    unnamed x69, local copies, waits for them, and re-layouts  19.4 us
  transfers between devices with their start and end apart: 16, of which 14 were waited for; matrix products, arithmetic and copies ran while one was open for 20% of the time, Pallas kernels for 0%

profile of v3, /device:TPU:0, one launch (start us, length us, event | category | flops | bytes accessed | tf_op | source)
XLA Modules:
  0.0 545.3 jit_solution(2286913383583947263)
XLA Ops:
  15.2 24.0 %all_gather.27 = bf16[1024,2,1,128]{3,0,1,2:T(8,128)(2,1)S(1)} all-gather(bf16[256,2,1,128]{3,0,1,2:T(8,128)(2,1)S(1)} %pad_maximum_fusion.1), channel_id=1, replica_groups=mesh['tensor'=4,'expert'=4,'dp'=2] {'expert'}, dimensions={0}, use_global_device_ids=true | all-gather | bytes 655360 | tf_op jit(solution)/shard_map/all_gather | solution.py:156
  39.2 22.1 %all-gather = bf16[1,1024,2,128]{3,1,2,0:T(8,128)(2,1)S(1)} all-gather(bf16[1,256,2,128]{3,1,2,0:T(8,128)(2,1)S(1)} %copy.85), channel_id=2, replica_groups=mesh['tensor'=4,'expert'=4,'dp'=2] {'expert'}, dimensions={1}, use_global_device_ids=true | all-gather | bytes 655360 | tf_op jit(solution)/shard_map/all_gather | solution.py:157
  61.3 29.2 %conditional.1 = (f32[2,1,8,256]{3,2,0,1:T(8,128)S(1)}, f32[2,1,8,256,128]{4,3,2,0,1:T(8,128)}) conditional(s32[]{:T(128)} %convert_element_type.310, () %tuple.18, (s32[1024]{0:T(1024)S(1)}, s32[256]{0:T(256)S(1)}, s32[1024]{0:T(1024)S(1)}, s32[]{:T(128)}, s32[1024]{0:T(1024)S(1)}, /*index=5*/bf16[1024,2,1,128]{3,0,1,2:T(8,128)(2,1)S(1)}, ...), branch_computations={%region_3.0_spmd, %region_4.7_spmd} | conditional | flops 2202793984 | bytes 55690260 | solution.py:77
  62.2 7.1 %fusion = (f32[2,8,256]{2,1,0:T(8,128)S(1)}, f32[2,1024,256,8]{2,1,3,0:T(8,128)}) fusion(pred[256,1024]{0,1:T(8,128)(4,1)S(1)} %and_and_fusion, bf16[256,2,1,8,128]{0,4,3,1,2:T(8,128)(2,1)S(1)} %get-tuple-element.73, bf16[1024,2,1,128]{3,0,1,2:T(8,128)(2,1)S(1)} %get-tuple-element.24), kind=kOutput, calls=%fused_computation.2 | convolution fusion | flops 1086320640 | bytes 18628608 | tf_op jit(solution)/shard_map/cond/branch_1_fun/pskgd,nskd->skgpn/dot_general | solution.py:50
  69.3 12.7 %fusion.7 = f32[2,1,8,256,128]{4,3,2,0,1:T(8,128)} fusion(f32[2,1024,256,8]{2,1,3,0:T(8,128)} %get-tuple-element.78, f32[2,8,256]{2,1,0:T(8,128)S(1)} %broadcast_maximum_fusion, pred[256,1024]{0,1:T(8,128)(4,1)S(1)} %and_and_fusion, bf16[1024,2,1,128]{3,0,1,2:T(8,128)(2,1)S(1)} %get-tuple-element.26), kind=kOutput, calls=%fused_computation.8 | convolution fusion | flops 1094713344 | bytes 19677184 | tf_op jit(solution)/shard_map/cond/branch_1_fun/skgpn,nskd->skgpd/dot_general | solution.py:64
  82.0 8.0 %fusion.2 = f32[2,8,256]{2,1,0:T(8,128)S(1)} fusion(f32[2,1024,256,8]{2,1,3,0:T(8,128)} %get-tuple-element.78, f32[2,8,256]{2,1,0:T(8,128)S(1)} %broadcast_maximum_fusion, pred[256,1024]{0,1:T(8,128)(4,1)S(1)} %and_and_fusion), kind=kLoop, calls=%fused_computation.4 | loop fusion | flops 20967424 | bytes 17072128 | tf_op jit(solution)/shard_map/cond/branch_1_fun/reduce_sum | solution.py:63
  93.6 32.5 %all_gather.29 = s32[16,128,8]{1,2,0:T(8,128)S(1)} all-gather(s32[1,128,8]{1,2,0:T(8,128)S(1)} %copy.89), channel_id=1, replica_groups=mesh['tensor'=4,'expert'=4,'dp'=2] {'tensor','expert'}, dimensions={0}, use_global_device_ids=true | all-gather | bytes 69632 | tf_op jit(solution)/shard_map/all_gather | solution.py:172
  126.1 26.1 %all-gather.8.cloned.1.call-done = bf16[8192,512]{1,0:T(8,128)(2,1)} async-done(((bf16[1024,512]{1,0:T(8,128)(2,1)}), bf16[8192,512]{1,0:T(8,128)(2,1)}) %all-gather.8.cloned.1.call-update) | async-done | bytes 8388624 | tf_op jit(solution)/shard_map/all_gather | solution.py:168
  168.6 6.4 %copy.103 = bf16[512,4096]{1,0:T(8,128)(2,1)} copy(bf16[512,4096]{0,1:T(8,128)(2,1)} %fusion.60) | data formatting | bytes 8388608
  176.6 41.3 %reduce-scatter.4.cloned.1.call-done = bf16[128,4096]{1,0:T(8,128)(2,1)} async-done(((bf16[512,4096]{1,0:T(8,128)(2,1)}), bf16[128,4096]{1,0:T(8,128)(2,1)}) %reduce-scatter.4.cloned.1.call-update) | async-done | bytes 1048592 | tf_op jit(solution)/shard_map/reduce_scatter | solution.py:183
  221.8 74.3 %all-gather.10.cloned.1.call-done = bf16[1024,4096]{1,0:T(8,128)(2,1)} async-done(((bf16[64,4096]{1,0:T(8,128)(2,1)}), bf16[1024,4096]{1,0:T(8,128)(2,1)}) %all-gather.10.cloned.1.call-update) | async-done | bytes 8388624 | tf_op jit(solution)/shard_map/all_gather | solution.py:207
  296.1 5.8 %select_reduce_fusion.1 = (f32[1024]{0:T(1024)S(1)}, f32[1024,16]{0,1:T(8,128)S(1)}) fusion(pred[1024,16]{0,1:T(8,128)(4,1)S(1)} %fusion.82, bf16[1024,4096]{1,0:T(8,128)(2,1)} %all-gather.10.cloned.1.call-done, bf16[4096,16]{0,1:T(8,128)(2,1)S(1)} %copy-done.11), kind=kOutput, calls=%fused_computation.133 | convolution fusion | flops 134249472 | bytes 8605696 | tf_op jit(solution)/shard_map/dot_general | solution.py:214
  302.0 9.4 %fusion.27 = f32[1024,768]{1,0:T(8,128)S(1)} fusion(bf16[1024,4096]{1,0:T(8,128)(2,1)S(1)} %copy-done.5, bf16[1,4096,768]{2,1,0:T(8,128)(2,1)} %param.26), kind=kOutput, calls=%fused_computation.34 | convolution fusion | flops 6442450944 | bytes 17825792 | tf_op jit(solution)/shard_map/dot_general | solution.py:221
  311.5 7.0 %multiply_convert_fusion.3 = bf16[1024,768]{1,0:T(8,128)(2,1)S(1)} fusion(f32[1024,768]{1,0:T(8,128)S(1)} %fusion.27, bf16[1024,4096]{1,0:T(8,128)(2,1)S(1)} %copy-done.5, bf16[1,4096,768]{2,1,0:T(8,128)(2,1)S(1)} %bitcast.225), kind=kOutput, calls=%fused_computation.50 | convolution fusion | flops 6447169536 | bytes 19398656 | tf_op jit(solution)/shard_map/dot_general | solution.py:220
  318.5 7.3 %multiply_convert_fusion = bf16[1024,4096]{1,0:T(8,128)(2,1)S(1)} fusion(f32[1024]{0:T(1024)S(1)} %select_reduce_fusion, bf16[1024,768]{1,0:T(8,128)(2,1)S(1)} %multiply_convert_fusion.3, bf16[1,768,4096]{2,1,0:T(8,128)(2,1)S(1)} %bitcast.231), kind=kOutput, calls=%fused_computation.20 | convolution fusion | flops 6459228160 | bytes 16257024 | tf_op jit(solution)/shard_map/dot_general | solution.py:225
  330.6 8.5 %collective-permute-done = bf16[2,4,64,4096]{3,2,1,0:T(8,128)(2,1)} collective-permute-done((bf16[2,4,64,4096]{3,2,1,0:T(8,128)(2,1)}, bf16[2,4,64,4096]{3,2,1,0:T(8,128)(2,1)}, u32[]{:S(2)}, u32[]{:S(2)}) %collective-permute-start) | collective-permute-done | bytes 4194336 | tf_op jit(solution)/shard_map/ppermute | solution.py:88
  339.1 5.1 fusion.17
  348.2 27.7 %all-gather.12.cloned.1.call-done = bf16[1024,4096]{1,0:T(8,128)(2,1)} async-done(((bf16[64,4096]{1,0:T(8,128)(2,1)}), bf16[1024,4096]{1,0:T(8,128)(2,1)}) %all-gather.12.cloned.1.call-update) | async-done | bytes 8388624 | tf_op jit(solution)/shard_map/all_gather | solution.py:207
  375.9 5.6 %fusion.94 = (bf16[16,32,4096]{2,1,0:T(8,128)(2,1)S(1)}, bf16[16,32,4096]{2,1,0:T(8,128)(2,1)}) fusion(bf16[16,64,4096]{2,1,0:T(8,128)(2,1)} %bitcast.199), kind=kLoop, calls=%fused_computation.158 | loop fusion | bytes 16777216 | tf_op jit(solution)/shard_map/slice | solution.py:209
  381.5 18.4 %collective-permute-done.1 = bf16[1,4,64,4096]{3,2,1,0:T(8,128)(2,1)} collective-permute-done((bf16[1,4,64,4096]{3,2,1,0:T(8,128)(2,1)S(1)}, bf16[1,4,64,4096]{3,2,1,0:T(8,128)(2,1)}, u32[]{:S(2)}, u32[]{:S(2)}) %collective-permute-start.1) | collective-permute-done | bytes 2097184 | tf_op jit(solution)/shard_map/ppermute | solution.py:88
  402.5 5.7 %fusion.31 = f32[512,768]{1,0:T(8,128)S(1)} fusion(bf16[512,4096]{1,0:T(8,128)(2,1)S(1)} %bitcast.192, bf16[1,4096,768]{2,1,0:T(8,128)(2,1)} %param.25), kind=kOutput, calls=%fused_computation.38 | convolution fusion | flops 3221225472 | bytes 12058624 | tf_op jit(solution)/shard_map/dot_general | solution.py:220
  409.6 3.5 multiply_convert_fusion.5
  413.1 3.6 multiply_convert_fusion.2
  428.5 5.9 %fusion.29 = f32[512,768]{1,0:T(8,128)S(1)} fusion(bf16[512,4096]{1,0:T(8,128)(2,1)S(1)} %bitcast.189, bf16[1,4096,768]{2,1,0:T(8,128)(2,1)} %param.25), kind=kOutput, calls=%fused_computation.36 | convolution fusion | flops 3221225472 | bytes 12058624 | tf_op jit(solution)/shard_map/dot_general | solution.py:220
  435.7 3.5 multiply_convert_fusion.4
  439.2 14.1 %collective-permute-done.5 = bf16[1,4,32,4096]{3,2,1,0:T(8,128)(2,1)S(1)} collective-permute-done((bf16[1,4,32,4096]{3,2,1,0:T(8,128)(2,1)S(1)}, bf16[1,4,32,4096]{3,2,1,0:T(8,128)(2,1)S(1)}, u32[]{:S(2)}, u32[]{:S(2)}) %collective-permute-start.5) | collective-permute-done | bytes 1048608 | tf_op jit(solution)/shard_map/ppermute | solution.py:88
  454.6 3.6 multiply_convert_fusion.1
  469.1 20.9 %collective-permute-done.3 = bf16[1,1,64,4096]{3,2,1,0:T(8,128)(2,1)S(1)} collective-permute-done((bf16[1,1,64,4096]{3,2,1,0:T(8,128)(2,1)S(1)}, bf16[1,1,64,4096]{3,2,1,0:T(8,128)(2,1)S(1)}, u32[]{:S(2)}, u32[]{:S(2)}) %collective-permute-start.3) | collective-permute-done | bytes 524320 | tf_op jit(solution)/shard_map/ppermute | solution.py:88
  490.8 3.2 collective-permute-done.9
  495.8 9.2 %collective-permute-done.6 = bf16[1,2,32,4096]{3,2,1,0:T(8,128)(2,1)S(1)} collective-permute-done((bf16[1,2,32,4096]{3,2,1,0:T(8,128)(2,1)S(1)}, bf16[1,2,32,4096]{3,2,1,0:T(8,128)(2,1)S(1)}, u32[]{:S(2)}, u32[]{:S(2)}) %collective-permute-start.6) | collective-permute-done | bytes 524320 | tf_op jit(solution)/shard_map/ppermute | solution.py:88
  507.1 13.6 %collective-permute-done.10 = bf16[1,2,32,4096]{3,2,1,0:T(8,128)(2,1)S(1)} collective-permute-done((bf16[1,2,32,4096]{3,2,1,0:T(8,128)(2,1)S(1)}, bf16[1,2,32,4096]{3,2,1,0:T(8,128)(2,1)S(1)}, u32[]{:S(2)}, u32[]{:S(2)}) %collective-permute-start.10) | collective-permute-done | bytes 524320 | tf_op jit(solution)/shard_map/ppermute | solution.py:88
  522.7 11.8 %collective-permute-done.11 = bf16[1,1,32,4096]{3,2,1,0:T(8,128)(2,1)S(1)} collective-permute-done((bf16[1,1,32,4096]{3,2,1,0:T(8,128)(2,1)S(1)}, bf16[1,1,32,4096]{3,2,1,0:T(8,128)(2,1)S(1)}, u32[]{:S(2)}, u32[]{:S(2)}) %collective-permute-start.11) | collective-permute-done | bytes 262176 | tf_op jit(solution)/shard_map/ppermute | solution.py:88
  (179 shorter events, 82.0 us)
Async XLA Ops:
  6.5 7.1 %copy-start.13 = (bf16[1,256,2,128]{3,2,1,0:T(2,128)(2,1)S(1)}, bf16[1,256,2,128]{3,2,1,0:T(2,128)(2,1)}, u32[]{:S(2)}) copy-start(bf16[1,256,2,128]{3,2,1,0:T(2,128)(2,1)} %param.16) | copy-start | bytes 393220
  6.5 7.3 %copy-start.17 = (f32[128]{0:T(128)S(1)}, f32[128]{0:T(128)}, u32[]{:S(2)}) copy-start(f32[128]{0:T(128)} %param.19) | copy-start | bytes 1540
  6.5 145.7 %all-gather.8.cloned.1.call-start = ((), (), s32[]{:S(2)}) async-start(), calls=%async_computation.1 | async-start | bytes 9437184 | tf_op jit(solution)/shard_map/all_gather | solution.py:168
  9.2 208.6 %reduce-scatter.4.cloned.1.call-start = ((), (), s32[]{:S(2)}) async-start(), calls=%async_computation.4 | async-start | bytes 5242880 | tf_op jit(solution)/shard_map/reduce_scatter | solution.py:183
  152.2 8.5 %copy-start.19 = (bf16[8192,512]{1,0:T(8,128)(2,1)S(1)}, bf16[8192,512]{1,0:T(8,128)(2,1)}, u32[]{:S(2)}) copy-start(bf16[8192,512]{1,0:T(8,128)(2,1)} %all-gather.8.cloned.1.call-done) | copy-start | bytes 25165828
  175.0 44.5 %copy-start.15 = (f32[4096]{0:T(1024)S(1)}, f32[4096]{0:T(1024)}, u32[]{:S(2)}) copy-start(f32[4096]{0:T(1024)} %param.22) | copy-start | bytes 49156
  175.0 121.0 %all-gather.10.cloned.1.call-start = ((), (), s32[]{:S(2)}) async-start(), calls=%async_computation.2 | async-start | bytes 8912896 | tf_op jit(solution)/shard_map/all_gather | solution.py:207
  176.6 119.5 %copy-start.11 = (bf16[4096,16]{0,1:T(8,128)(2,1)S(1)}, bf16[4096,16]{0,1:T(8,128)(2,1)}, u32[]{:S(2)}) copy-start(bf16[4096,16]{0,1:T(8,128)(2,1)} %param.23) | copy-start | bytes 393220
  221.0 154.9 %all-gather.12.cloned.1.call-start = ((), (), s32[]{:S(2)}) async-start(), calls=%async_computation.3 | async-start | bytes 8912896 | tf_op jit(solution)/shard_map/all_gather | solution.py:207
  296.1 15.4 %slice-start = ((s8[6291456]{0:T(1024)(128)(4,1)}), s8[4194304]{0:T(1024)(128)(4,1)S(1)}, s32[]{:S(2)}) async-start(s8[6291456]{0:T(1024)(128)(4,1)} %bitcast.224), calls=%async_computation.5 | async-start | bytes 8388608
  302.0 9.5 %slice-start.1 = ((s8[6291456]{0:T(1024)(128)(4,1)}), s8[2097152]{0:T(1024)(128)(4,1)S(1)}, s32[]{:S(2)}) async-start(s8[6291456]{0:T(1024)(128)(4,1)} %bitcast.224), calls=%async_computation.6 | async-start | bytes 4194304
  302.0 16.5 %slice-start.6 = ((s8[6291456]{0:T(1024)(128)(4,1)}), s8[4194304]{0:T(1024)(128)(4,1)S(1)}, s32[]{:S(2)}) async-start(s8[6291456]{0:T(1024)(128)(4,1)} %bitcast.230), calls=%async_computation.11 | async-start | bytes 8388608
  330.3 8.7 %collective-permute-start = (bf16[2,4,64,4096]{3,2,1,0:T(8,128)(2,1)}, bf16[2,4,64,4096]{3,2,1,0:T(8,128)(2,1)}, u32[]{:S(2)}, u32[]{:S(2)}) collective-permute-start(bf16[2,4,64,4096]{3,2,1,0:T(8,128)(2,1)} %dynamic-slice_bitcast_fusion), channel_id=1, source_target_pairs={{0,8},{8,0},{16,24},{24,16},{1,9},{9,1},{17,25},{25,17},{2,10},{10... | collective-permute-start | bytes 12582920 | tf_op jit(solution)/shard_map/ppermute | solution.py:88
  346.2 53.7 %collective-permute-start.1 = (bf16[1,4,64,4096]{3,2,1,0:T(8,128)(2,1)S(1)}, bf16[1,4,64,4096]{3,2,1,0:T(8,128)(2,1)}, u32[]{:S(2)}, u32[]{:S(2)}) collective-permute-start(bf16[1,4,64,4096]{3,2,1,0:T(8,128)(2,1)S(1)} %constant_dynamic-slice_fusion.5), channel_id=1, source_target_pairs={{0,16},{8,24},{16,0},{24,8},{1,17},{9,25},{17,1},{25,9},{2,18},{10... | collective-permute-start | bytes 6291464 | tf_op jit(solution)/shard_map/ppermute | solution.py:88
  375.9 24.0 %copy-start.3 = (bf16[2,4,64,4096]{3,2,1,0:T(8,128)(2,1)S(1)}, bf16[2,4,64,4096]{3,2,1,0:T(8,128)(2,1)}, u32[]{:S(2)}) copy-start(bf16[2,4,64,4096]{3,2,1,0:T(8,128)(2,1)} %copy-done.2) | copy-start | bytes 12582916
  399.9 9.6 %slice-start.2 = ((s8[6291456]{0:T(1024)(128)(4,1)}), s8[2097152]{0:T(1024)(128)(4,1)S(1)}, s32[]{:S(2)}) async-start(s8[6291456]{0:T(1024)(128)(4,1)} %bitcast.226), calls=%async_computation.7 | async-start | bytes 4194304
  420.3 4.5 collective-permute-start.4
  421.6 40.2 %collective-permute-start.2 = (bf16[1,2,64,4096]{3,2,1,0:T(8,128)(2,1)}, bf16[1,2,64,4096]{3,2,1,0:T(8,128)(2,1)}, u32[]{:S(2)}, u32[]{:S(2)}) collective-permute-start(bf16[1,2,64,4096]{3,2,1,0:T(8,128)(2,1)} %dynamic-slice_bitcast_fusion.3), channel_id=1, source_target_pairs={{0,2},{2,0},{4,6},{6,4},{1,3},{3,1},{5,7},{7,5},{8,10},{10,8},{12,... | collective-permute-start | bytes 3145736 | tf_op jit(solution)/shard_map/ppermute | solution.py:88
  424.8 10.9 %slice-start.4 = ((s8[6291456]{0:T(1024)(128)(4,1)}), s8[4194304]{0:T(1024)(128)(4,1)S(1)}, s32[]{:S(2)}) async-start(s8[6291456]{0:T(1024)(128)(4,1)} %bitcast.228), calls=%async_computation.9 | async-start | bytes 8388608
  428.1 25.3 %collective-permute-start.5 = (bf16[1,4,32,4096]{3,2,1,0:T(8,128)(2,1)S(1)}, bf16[1,4,32,4096]{3,2,1,0:T(8,128)(2,1)S(1)}, u32[]{:S(2)}, u32[]{:S(2)}) collective-permute-start(bf16[1,4,32,4096]{3,2,1,0:T(8,128)(2,1)S(1)} %constant_dynamic-slice_fusion.3), channel_id=1, source_target_pairs={{0,16},{8,24},{16,0},{24,8},{1,17},{9,25},{17,1},{25,9},{2,18},{10... | collective-permute-start | bytes 3145736 | tf_op jit(solution)/shard_map/ppermute | solution.py:88
  428.5 7.3 %slice-start.5 = ((s8[6291456]{0:T(1024)(128)(4,1)}), s8[2097152]{0:T(1024)(128)(4,1)S(1)}, s32[]{:S(2)}) async-start(s8[6291456]{0:T(1024)(128)(4,1)} %bitcast.228), calls=%async_computation.10 | async-start | bytes 4194304
  428.5 26.1 %slice-start.10 = ((s8[6291456]{0:T(1024)(128)(4,1)}), s8[4194304]{0:T(1024)(128)(4,1)S(1)}, s32[]{:S(2)}) async-start(s8[6291456]{0:T(1024)(128)(4,1)} %bitcast.234), calls=%async_computation.15 | async-start | bytes 8388608
  434.4 20.2 %slice-start.11 = ((s8[6291456]{0:T(1024)(128)(4,1)}), s8[2097152]{0:T(1024)(128)(4,1)S(1)}, s32[]{:S(2)}) async-start(s8[6291456]{0:T(1024)(128)(4,1)} %bitcast.234), calls=%async_computation.16 | async-start | bytes 4194304
  461.8 4.5 collective-permute-start.8
  463.5 26.7 %copy-start.10 = (bf16[1,4,32,4096]{3,2,1,0:T(8,128)(2,1)S(1)}, bf16[1,4,32,4096]{3,2,1,0:T(8,128)(2,1)}, u32[]{:S(2)}) copy-start(bf16[1,4,32,4096]{3,2,1,0:T(8,128)(2,1)} %add_convert_fusion.2) | copy-start | bytes 3145732
  463.5 26.5 %collective-permute-start.3 = (bf16[1,1,64,4096]{3,2,1,0:T(8,128)(2,1)S(1)}, bf16[1,1,64,4096]{3,2,1,0:T(8,128)(2,1)S(1)}, u32[]{:S(2)}, u32[]{:S(2)}) collective-permute-start(bf16[1,1,64,4096]{3,2,1,0:T(8,128)(2,1)S(1)} %constant_dynamic-slice_fusion.4), channel_id=1, source_target_pairs={{0,4},{2,6},{4,0},{6,2},{1,5},{3,7},{5,1},{7,3},{8,12},{10,14},{12... | collective-permute-start | bytes 1572872 | tf_op jit(solution)/shard_map/ppermute | solution.py:88
  468.7 25.3 %collective-permute-start.9 = (bf16[1,4,32,4096]{3,2,1,0:T(8,128)(2,1)S(1)}, bf16[1,4,32,4096]{3,2,1,0:T(8,128)(2,1)S(1)}, u32[]{:S(2)}, u32[]{:S(2)}) collective-permute-start(bf16[1,4,32,4096]{3,2,1,0:T(8,128)(2,1)S(1)} %constant_dynamic-slice_fusion.1), channel_id=1, source_target_pairs={{0,16},{8,24},{16,0},{24,8},{1,17},{9,25},{17,1},{25,9},{2,18},{10... | collective-permute-start | bytes 3145736 | tf_op jit(solution)/shard_map/ppermute | solution.py:88
  490.2 14.9 %collective-permute-start.6 = (bf16[1,2,32,4096]{3,2,1,0:T(8,128)(2,1)S(1)}, bf16[1,2,32,4096]{3,2,1,0:T(8,128)(2,1)S(1)}, u32[]{:S(2)}, u32[]{:S(2)}) collective-permute-start(bf16[1,2,32,4096]{3,2,1,0:T(8,128)(2,1)S(1)} %dynamic-slice_bitcast_fusion.5), channel_id=1, source_target_pairs={{0,2},{2,0},{4,6},{6,4},{1,3},{3,1},{5,7},{7,5},{8,10},{10,8},{12,... | collective-permute-start | bytes 1572872 | tf_op jit(solution)/shard_map/ppermute | solution.py:88
  494.3 26.4 %collective-permute-start.10 = (bf16[1,2,32,4096]{3,2,1,0:T(8,128)(2,1)S(1)}, bf16[1,2,32,4096]{3,2,1,0:T(8,128)(2,1)S(1)}, u32[]{:S(2)}, u32[]{:S(2)}) collective-permute-start(bf16[1,2,32,4096]{3,2,1,0:T(8,128)(2,1)S(1)} %dynamic-slice_bitcast_fusion.4), channel_id=1, source_target_pairs={{0,2},{2,0},{4,6},{6,4},{1,3},{3,1},{5,7},{7,5},{8,10},{10,8},{12,... | collective-permute-start | bytes 1572872 | tf_op jit(solution)/shard_map/ppermute | solution.py:88
  505.2 33.1 %copy-start.1 = (bf16[1024,1024]{1,0:T(8,128)(2,1)S(1)}, bf16[1024,1024]{1,0:T(8,128)(2,1)}, u32[]{:S(2)}) copy-start(bf16[1024,1024]{1,0:T(8,128)(2,1)} %param.20) | copy-start | bytes 6291460
  505.3 17.4 %collective-permute-start.7 = (bf16[1,1,32,4096]{3,2,1,0:T(8,128)(2,1)S(1)}, bf16[1,1,32,4096]{3,2,1,0:T(8,128)(2,1)S(1)}, u32[]{:S(2)}, u32[]{:S(2)}) collective-permute-start(bf16[1,1,32,4096]{3,2,1,0:T(8,128)(2,1)S(1)} %constant_dynamic-slice_fusion.2), channel_id=1, source_target_pairs={{0,4},{2,6},{4,0},{6,2},{1,5},{3,7},{5,1},{7,3},{8,12},{10,14},{12... | collective-permute-start | bytes 786440 | tf_op jit(solution)/shard_map/ppermute | solution.py:88
  520.8 13.6 %collective-permute-start.11 = (bf16[1,1,32,4096]{3,2,1,0:T(8,128)(2,1)S(1)}, bf16[1,1,32,4096]{3,2,1,0:T(8,128)(2,1)S(1)}, u32[]{:S(2)}, u32[]{:S(2)}) collective-permute-start(bf16[1,1,32,4096]{3,2,1,0:T(8,128)(2,1)S(1)} %constant_dynamic-slice_fusion), channel_id=1, source_target_pairs={{0,4},{2,6},{4,0},{6,2},{1,5},{3,7},{5,1},{7,3},{8,12},{10,14},{12... | collective-permute-start | bytes 786440 | tf_op jit(solution)/shard_map/ppermute | solution.py:88
  (16 other events, 68.6 us)
Sparse Core Ops, SparseCore 0:
  9.5 142.6 all-gather.7
  175.2 42.6 reduce-scatter.3
  221.1 74.8 all-gather.9
  298.4 77.4 all-gather.11
